TPU v7x, 128 devices: a whole 4x4x4 slice. The times are simulated.
128 devices in a mesh: narrow: 8 (over y, core), wide: 16 (over x, z).
Axes of the slice: x: 4, y: 4, z: 4, core: 2. Of those that a mesh axis runs over, the one named last changes fastest.
Arguments:
- velocity: float32 [3, 256, 512, 1024], P(None, 'wide', 'narrow'), may hold values from -6 to 6
- exponents: int32 [7], replicated, may hold values from -1 to 2
Outputs:
- approx: float32 [3, 128, 256, 512], P(None, None, 'narrow', 'wide')
- details: float32 [3, 7, 128, 256, 512], P(None, None, 'wide', 'narrow')
All inputs are finite; a program needn't handle non-finite values.
Results may differ from a plain program's by a relative error of at most 0.000082.
Values sent between devices are 32-bit elements; how exact they have to be, the bound alone decides.
A program may use at most 256 MiB of HBM per device.

v0:
```python
import jax
import jax.numpy as jnp
from jax import lax
from jax.sharding import PartitionSpec as P

predict_one = -1.586134342
update_one = -0.05298011854
predict_two = 0.8829110762
update_two = 0.4435068522
scaling = 1.149604398
inverse_scaling = 1.0 / 1.149604398


def shifted(value, axis, by):
    length = lax.axis_size(axis)
    pairs = [(i, i + by) for i in range(length) if 0 <= i + by < length]
    return lax.ppermute(value, axis, pairs)


def with_halo(cells, sides, width):
    for axis, dim in sides:
        count = lax.axis_size(axis)
        ends = count - 1
        head = lax.slice_in_dim(cells, 0, width, axis=dim)
        tail = lax.slice_in_dim(cells, cells.shape[dim] - width, cells.shape[dim], axis=dim)
        cells = jnp.concatenate(
            [
                lax.ppermute(tail, axis, [(i, (i + 1) % count) for i in range(ends)]),
                cells,
                lax.ppermute(head, axis, [((i + 1) % count, i) for i in range(ends)]),
            ],
            axis=dim,
        )
    return cells


def cut_range(block_data, begin_at, end_at, dimension):
    return lax.slice_in_dim(block_data, begin_at, end_at, 1, dimension)


def lift_extended(extended, dimension):
    length = extended.shape[dimension]
    pair_count = length // 2
    even_part = lax.slice_in_dim(extended, 0, length, 2, dimension)
    odd_part = lax.slice_in_dim(extended, 1, length, 2, dimension)
    odd_part = cut_range(odd_part, 0, pair_count - 1, dimension) + predict_one * (
        cut_range(even_part, 0, pair_count - 1, dimension)
        + cut_range(even_part, 1, pair_count, dimension)
    )
    even_part = cut_range(even_part, 1, pair_count - 1, dimension) + update_one * (
        cut_range(odd_part, 0, pair_count - 2, dimension)
        + cut_range(odd_part, 1, pair_count - 1, dimension)
    )
    odd_part = cut_range(odd_part, 1, pair_count - 2, dimension) + predict_two * (
        cut_range(even_part, 0, pair_count - 3, dimension)
        + cut_range(even_part, 1, pair_count - 2, dimension)
    )
    even_part = cut_range(even_part, 1, pair_count - 3, dimension) + update_two * (
        cut_range(odd_part, 0, pair_count - 4, dimension)
        + cut_range(odd_part, 1, pair_count - 3, dimension)
    )
    return (
        even_part * scaling,
        cut_range(odd_part, 1, pair_count - 3, dimension) * inverse_scaling,
    )


def mirror_rim(extended, dimension, at_first, at_last):
    inner = extended.shape[dimension] - 8
    head = jnp.where(
        at_first,
        jnp.flip(cut_range(extended, 5, 9, dimension), dimension),
        cut_range(extended, 0, 4, dimension),
    )
    tail = jnp.where(
        at_last,
        jnp.flip(cut_range(extended, inner - 1, inner + 3, dimension), dimension),
        cut_range(extended, inner + 4, inner + 8, dimension),
    )
    return jnp.concatenate([head, cut_range(extended, 4, inner + 4, dimension), tail], dimension)


def lift_steps(block_data, dimension, from_right, from_left):
    length = block_data.shape[dimension]
    half_count = length // 2
    even_part = lax.slice_in_dim(block_data, 0, length, 2, dimension)
    odd_part = lax.slice_in_dim(block_data, 1, length, 2, dimension)

    def single(part, position):
        return cut_range(part, position, position + 1, dimension)

    for predict, update in ((predict_one, update_one), (predict_two, update_two)):
        following = from_right(single(even_part, 0), single(even_part, half_count - 1))
        odd_part = odd_part + predict * (
            even_part
            + jnp.concatenate(
                [cut_range(even_part, 1, half_count, dimension), following], dimension
            )
        )
        preceding = from_left(single(odd_part, half_count - 1), single(odd_part, 0))
        even_part = even_part + update * (
            jnp.concatenate(
                [preceding, cut_range(odd_part, 0, half_count - 1, dimension)], dimension
            )
            + odd_part
        )
    return (even_part * scaling, odd_part * inverse_scaling)


def right_wide(first_cell, last_cell):
    fetched = shifted(first_cell, "wide", -1)
    return jnp.where(lax.axis_index("wide") == lax.axis_size("wide") - 1, last_cell, fetched)


def left_wide(last_cell, first_cell):
    fetched = shifted(last_cell, "wide", 1)
    return jnp.where(lax.axis_index("wide") == 0, first_cell, fetched)


def lift_matrix(length, padded):
    identity = jnp.eye(length, dtype=jnp.float32)
    if padded:
        identity = jnp.pad(identity, ((0, 0), (4, 4)), mode="reflect")
    low_part, high_part = lift_extended(identity, 1)
    return jnp.concatenate([low_part, high_part], 1)


def local(velocity, exponents):
    first_narrow = lax.axis_index("narrow") == 0
    last_narrow = lax.axis_index("narrow") == lax.axis_size("narrow") - 1
    low_x, high_x = lift_steps(velocity, 1, right_wide, left_wide)
    stacked = jnp.stack([low_x, high_x], 1)
    depth = stacked.shape[4]
    z_matrix = lift_matrix(depth, True)
    along_z = jnp.dot(
        stacked.reshape((-1, depth)),
        z_matrix,
        precision=lax.Precision.HIGHEST,
        preferred_element_type=jnp.float32,
    ).reshape(stacked.shape)
    extended = with_halo(along_z, (("narrow", 3),), 4)
    extended = mirror_rim(extended, 3, first_narrow, last_narrow)
    y_matrix = lift_matrix(extended.shape[3], False)
    along_y = jnp.einsum(
        "yk,abcyz->abckz",
        y_matrix,
        extended,
        precision=lax.Precision.HIGHEST,
        preferred_element_type=jnp.float32,
    )
    half_x = along_y.shape[2]
    half_y = along_y.shape[3] // 2
    half_z = depth // 2
    split = along_y.reshape((3, 2, half_x, 2, half_y, 2, half_z))
    octants = jnp.transpose(split, (0, 1, 3, 5, 2, 4, 6)).reshape((3, 8, half_x, half_y, half_z))
    relaid = lax.all_to_all(octants[:, 0], "wide", split_axis=3, concat_axis=1, tiled=True)
    step_sizes = jnp.exp2(exponents.astype(jnp.float32))
    scaled = octants[:, 1:] / step_sizes[None, :, None, None, None]
    return (relaid, scaled - jnp.clip(scaled, -0.5, 0.5))


def solution(mesh):
    placed = (P(None, "wide", "narrow", None), P())
    return jax.shard_map(
        local,
        mesh=mesh,
        in_specs=placed,
        out_specs=(P(None, None, "narrow", "wide"), P(None, None, "wide", "narrow", None)),
        check_vma=False,
    )
```

profile of v0, /device:TPU:24, one launch (start us, length us, event | category | flops | bytes accessed | tf_op | source)
XLA Modules:
  0.0 504.8 jit_solution(13942489118191598349)
XLA Ops:
  9.6 15.9 %collective-permute-done = f32[3,1,64,1024]{3,2,1,0:T(8,128)S(1)} collective-permute-done((f32[3,1,64,1024]{3,2,1,0:T(8,128)S(1)}, f32[3,1,64,1024]{3,2,1,0:T(8,128)S(1)}, u32[]{:S(2)}, u32[]{:S(2)}) %collective-permute-start) | collective-permute-done | bytes 786464 | tf_op jit(solution)/shard_map/ppermute | solution.py:17
  26.7 7.4 %fusion.11 = f32[3,8,64,1024]{3,2,1,0:T(8,128)S(1)} fusion(f32[3,1,64,1024]{3,2,1,0:T(8,128)S(1)} %slice_select_fusion.3, f32[3,7,64,1024]{3,2,1,0:T(8,128)} %slice.228, f32[3,16,64,1024]{3,2,1,0:T(8,128)} %param.2), kind=kLoop, calls=%fused_computation.15 | loop fusion | flops 6291456 | bytes 25165824 | tf_op jit(solution)/shard_map/add | solution.py:94
  37.7 3.9 collective-permute-start.1
  45.8 6.4 %concatenate.29 = f32[1024,1032]{1,0:T(8,128)} concatenate(f32[1024,4]{1,0:T(8,128)S(1)} %rev.16, f32[1024,1024]{1,0:T(8,128)} %copy-done.3, f32[1024,4]{1,0:T(8,128)S(1)} %rev.17), dimensions={1} | concatenate | bytes 8454144 | tf_op jit(solution)/shard_map/jit(_pad)/concatenate | solution.py:123
  52.2 74.3 %slice.194 = f32[1024,516]{1,0:T(8,128)} slice(f32[1024,1032]{1,0:T(8,128)} %concatenate.29), slice={[0:1024:1], [0:1032:2]} | slice | bytes 4227072 | tf_op jit(solution)/shard_map/slice | solution.py:44
  126.5 74.5 %slice.196 = f32[1024,516]{1,0:T(8,128)} slice(f32[1024,1032]{1,0:T(8,128)} %concatenate.29), slice={[0:1024:1], [1:1032:2]} | slice | bytes 4227072 | tf_op jit(solution)/shard_map/slice | solution.py:45
  205.0 4.3 fusion.13
  214.5 15.1 %collective-permute-done.2 = f32[3,1,64,1024]{3,2,1,0:T(8,128)S(1)} collective-permute-done((f32[3,1,64,1024]{3,2,1,0:T(8,128)S(1)}, f32[3,1,64,1024]{3,2,1,0:T(8,128)S(1)}, u32[]{:S(2)}, u32[]{:S(2)}) %collective-permute-start.2) | collective-permute-done | bytes 786464 | tf_op jit(solution)/shard_map/ppermute | solution.py:17
  229.7 5.8 %multiply_bitcast_fusion = (f32[3,1,8,64,1024]{4,3,2,1,0:T(8,128)}, f32[3,8,64,1024]{3,2,1,0:T(8,128)}) fusion(f32[3,8,64,1024]{3,2,1,0:T(8,128)S(1)} %bitcast.42, f32[3,8,64,1024]{3,2,1,0:T(8,128)S(1)} %fusion.13, f32[3,1,64,1024]{3,2,1,0:T(8,128)S(1)} %slice_select_fusion.1, f32[3,7,64,1024]{3,2,1,0:T(8,128)S(1)} %slice.234), kind=kLoop, calls=%fused_computation.27 | loop fusion | flops 7864320 | bytes 31457280 | tf_op jit(solution)/shard_map/stack | solution.py:132
  236.7 5.4 %collective-permute-start.3 = (f32[3,1,64,1024]{3,2,1,0:T(8,128)S(1)}, f32[3,1,64,1024]{3,2,1,0:T(8,128)S(1)}, u32[]{:S(2)}, u32[]{:S(2)}) collective-permute-start(f32[3,1,64,1024]{3,2,1,0:T(8,128)S(1)} %slice.238), channel_id=1, source_target_pairs={{0,1},{1,2},{2,3},{3,4},{4,5},{5,6},{6,7},{7,8},{8,9},{9,10},{10,1... | collective-permute-start | bytes 2359304 | tf_op jit(solution)/shard_map/ppermute | solution.py:17
  246.7 10.5 %collective-permute-done.3 = f32[3,1,64,1024]{3,2,1,0:T(8,128)S(1)} collective-permute-done((f32[3,1,64,1024]{3,2,1,0:T(8,128)S(1)}, f32[3,1,64,1024]{3,2,1,0:T(8,128)S(1)}, u32[]{:S(2)}, u32[]{:S(2)}) %collective-permute-start.3) | collective-permute-done | bytes 786464 | tf_op jit(solution)/shard_map/ppermute | solution.py:17
  259.6 43.5 %fusion.6 = f32[3,2,8,64,1024]{4,3,2,1,0:T(8,128)S(1)} fusion(f32[3,1,8,64,1024]{4,3,2,1,0:T(8,128)} %get-tuple-element.6, f32[3,1,8,64,1024]{4,3,2,1,0:T(8,128)S(1)} %fusion.19, f32[1024,512]{1,0:T(8,128)S(1)} %copy-done.5, f32[1024,512]{1,0:T(8,128)S(1)} %get-tuple-element.14), kind=kOutput, calls=%fused_computation.8 | convolution fusion | flops 38658899968 | bytes 29360128 | tf_op jit(solution)/shard_map/dot_general | solution.py:135
  312.8 3.9 collective-permute-done.5
  321.5 21.1 %fusion.20 = f32[3,2,8,64,1024]{4,3,2,1,0:T(8,128)} fusion(f32[3,2,8,4,1024]{4,3,2,1,0:T(4,128)S(1)} %bitcast.50, f32[3,2,8,64,1024]{4,3,2,1,0:T(8,128)} %copy-done.6, f32[3,2,8,4,1024]{4,3,2,1,0:T(4,128)S(1)} %bitcast.51, f32[72,32]{0,1:T(8,128)S(1)} %get-tuple-element.17, f32[72,32]{0,1:T(8,128)S(1)} %get-tuple-element.16), kind=kOutput, calls=%fused_computation.28 | convolution fusion | flops 2724991488 | bytes 26757120 | tf_op jit(solution)/shard_map/yk,abcyz->abckz/dot_general | solution.py:144
  342.6 16.9 %reshape.15 = f32[3,2,8,2,32,2,512]{6,5,4,3,2,1,0:T(2,128)} reshape(f32[3,2,8,64,1024]{4,3,2,1,0:T(8,128)} %fusion.20) | data formatting | bytes 25165824 | tf_op jit(solution)/shard_map/reshape | solution.py:154
  359.5 41.1 %copy.12 = f32[3,2,2,2,8,32,512]{5,4,0,6,3,2,1:T(8,128)} copy(f32[3,2,2,2,8,32,512]{6,3,5,2,4,1,0:T(2,128)} %bitcast.45) | data formatting | bytes 25165824 | tf_op jit(solution)/shard_map/transpose | solution.py:155
  400.5 5.9 %fusion.52 = f32[512,3,8,32]{3,2,1,0:T(8,128)} fusion(f32[3,8,8,32,512]{3,2,0,4,1:T(8,128)} %bitcast.39), kind=kLoop, calls=%fused_computation.78 | loop fusion | bytes 3145728
  406.4 5.9 %reshape.19 = f32[16,1,24576]{2,1,0:T(1,128)} reshape(f32[512,3,8,32]{3,2,1,0:T(8,128)} %fusion.52) | data formatting | bytes 3145728
  412.3 9.3 %all-to-all-start = ((f32[16,1,24576]{2,1,0:T(1,128)}), f32[16,1,24576]{2,1,0:T(1,128)S(1)}, u32[]{:S(2)}, u32[]{:S(2)}) async-start(f32[16,1,24576]{2,1,0:T(1,128)} %reshape.19), calls=%async_computation | async-start | bytes 3145728 | tf_op jit(solution)/shard_map/all_to_all | solution.py:156
  421.6 32.3 %clamp_subtract_fusion = f32[3,7,8,32,512]{3,2,0,4,1:T(8,128)} fusion(f32[3,8,8,32,512]{3,2,0,4,1:T(8,128)} %bitcast.40, f32[7]{0:T(128)S(1)} %multiply_exponential_fusion), kind=kLoop, calls=%fused_computation | loop fusion | flops 8257536 | bytes 22020124 | tf_op jit(solution)/shard_map/sub | solution.py:159
  453.9 28.8 %copy.15 = f32[3,7,8,32,512]{4,3,2,1,0:T(8,128)} copy(f32[3,7,8,32,512]{3,2,0,4,1:T(8,128)} %clamp_subtract_fusion) | data formatting | bytes 22020096
  483.2 4.4 reduce
  491.4 6.6 %copy.13 = f32[3,8,32,16,32]{4,2,1,3,0:T(8,128)} copy(f32[3,8,32,16,32]{2,1,0,4,3:T(8,128)} %bitcast.46) | data formatting | bytes 3145728 | tf_op jit(solution)/shard_map/all_to_all | solution.py:156
  498.0 6.3 %copy.14 = f32[3,128,32,32]{1,3,2,0:T(8,128)} copy(f32[3,128,32,32]{3,2,1,0:T(8,128)} %bitcast.47) | data formatting | bytes 3145728
  (71 shorter events, 53.9 us)
Async XLA Ops:
  4.0 2.7 copy-start.2
  4.1 21.4 %collective-permute-start = (f32[3,1,64,1024]{3,2,1,0:T(8,128)S(1)}, f32[3,1,64,1024]{3,2,1,0:T(8,128)S(1)}, u32[]{:S(2)}, u32[]{:S(2)}) collective-permute-start(f32[3,1,64,1024]{3,2,1,0:T(8,128)S(1)} %slice.230), channel_id=1, source_target_pairs={{1,0},{2,1},{3,2},{4,3},{5,4},{6,5},{7,6},{8,7},{9,8},{10,9},{11,1... | collective-permute-start | bytes 2359304 | tf_op jit(solution)/shard_map/ppermute | solution.py:17
  34.1 2.7 copy-start
  37.7 163.5 %collective-permute-start.1 = (f32[3,1,64,1024]{3,2,1,0:T(8,128)}, f32[3,1,64,1024]{3,2,1,0:T(8,128)S(1)}, u32[]{:S(2)}, u32[]{:S(2)}) collective-permute-start(f32[3,1,64,1024]{3,2,1,0:T(8,128)} %slice.232), channel_id=1, source_target_pairs={{0,1},{1,2},{2,3},{3,4},{4,5},{5,6},{6,7},{7,8},{8,9},{9,10},{10,1... | collective-permute-start | bytes 2359304 | tf_op jit(solution)/shard_map/ppermute | solution.py:17
  42.1 2.0 copy-start.3
  126.5 74.7 %slice-start = ((s8[6291456]{0:T(1024)(128)(4,1)}), s8[2097152]{0:T(1024)(128)(4,1)S(1)}, s32[]{:S(2)}) async-start(s8[6291456]{0:T(1024)(128)(4,1)} %bitcast.41), calls=%async_computation.1 | async-start | bytes 4194304
  201.2 2.2 slice-start.1
  201.2 3.8 slice-start.2
  205.0 6.1 %copy-start.1 = (f32[1024,516]{1,0:T(8,128)S(1)}, f32[1024,516]{1,0:T(8,128)}, u32[]{:S(2)}) copy-start(f32[1024,516]{1,0:T(8,128)} %slice.194) | copy-start | bytes 6340612
  205.0 6.1 %copy-start.4 = (f32[1024,516]{1,0:T(8,128)S(1)}, f32[1024,516]{1,0:T(8,128)}, u32[]{:S(2)}) copy-start(f32[1024,516]{1,0:T(8,128)} %slice.196) | copy-start | bytes 6340612
  209.3 20.2 %collective-permute-start.2 = (f32[3,1,64,1024]{3,2,1,0:T(8,128)S(1)}, f32[3,1,64,1024]{3,2,1,0:T(8,128)S(1)}, u32[]{:S(2)}, u32[]{:S(2)}) collective-permute-start(f32[3,1,64,1024]{3,2,1,0:T(8,128)S(1)} %slice.236), channel_id=1, source_target_pairs={{1,0},{2,1},{3,2},{4,3},{5,4},{6,5},{7,6},{8,7},{9,8},{10,9},{11,1... | collective-permute-start | bytes 2359304 | tf_op jit(solution)/shard_map/ppermute | solution.py:17
  236.7 20.4 %collective-permute-start.3 = (f32[3,1,64,1024]{3,2,1,0:T(8,128)S(1)}, f32[3,1,64,1024]{3,2,1,0:T(8,128)S(1)}, u32[]{:S(2)}, u32[]{:S(2)}) collective-permute-start(f32[3,1,64,1024]{3,2,1,0:T(8,128)S(1)} %slice.238), channel_id=1, source_target_pairs={{0,1},{1,2},{2,3},{3,4},{4,5},{5,6},{6,7},{7,8},{8,9},{9,10},{10,1... | collective-permute-start | bytes 2359304 | tf_op jit(solution)/shard_map/ppermute | solution.py:17
  242.2 4.0 slice-start.3
  243.6 2.6 slice-start.4
  257.2 2.3 copy-start.5
  303.1 7.2 %copy-start.6 = (f32[3,2,8,64,1024]{4,3,2,1,0:T(8,128)}, f32[3,2,8,64,1024]{4,3,2,1,0:T(8,128)S(1)}, u32[]{:S(2)}) copy-start(f32[3,2,8,64,1024]{4,3,2,1,0:T(8,128)S(1)} %fusion.6) | copy-start | bytes 37748740
  303.1 7.2 %copy-start.7 = (s32[7]{0:T(128)S(1)}, s32[7]{0:T(128)}, u32[]{:S(2)}) copy-start(s32[7]{0:T(128)} %param.3) | copy-start | bytes 88
  305.0 11.7 %collective-permute-start.5 = (f32[3,2,8,4,1024]{4,3,2,1,0:T(4,128)}, f32[3,2,8,4,1024]{4,3,2,1,0:T(4,128)}, u32[]{:S(2)}, u32[]{:S(2)}) collective-permute-start(f32[3,2,8,4,1024]{4,3,2,1,0:T(4,128)} %get-tuple-element.9), channel_id=1, source_target_pairs={{16,0},{32,16},{48,32},{64,48},{80,64},{96,80},{112,96},{17,1},{33... | collective-permute-start | bytes 2359304 | tf_op jit(solution)/shard_map/ppermute | solution.py:30
  306.9 13.4 %collective-permute-start.4 = (f32[3,2,8,4,1024]{4,3,2,1,0:T(4,128)S(1)}, f32[3,2,8,4,1024]{4,3,2,1,0:T(4,128)}, u32[]{:S(2)}, u32[]{:S(2)}) collective-permute-start(f32[3,2,8,4,1024]{4,3,2,1,0:T(4,128)S(1)} %get-tuple-element.8), channel_id=1, source_target_pairs={{0,16},{16,32},{32,48},{48,64},{64,80},{80,96},{96,112},{1,17},{17... | collective-permute-start | bytes 2359304 | tf_op jit(solution)/shard_map/ppermute | solution.py:28
  412.3 70.4 %all-to-all-start = ((f32[16,1,24576]{2,1,0:T(1,128)}), f32[16,1,24576]{2,1,0:T(1,128)S(1)}, u32[]{:S(2)}, u32[]{:S(2)}) async-start(f32[16,1,24576]{2,1,0:T(1,128)} %reshape.19), calls=%async_computation | async-start | bytes 3145728 | tf_op jit(solution)/shard_map/all_to_all | solution.py:156
where the time goes:
time: 515 us; the launch traced here: 505 us
  local copies, waits for them, and re-layouts  297 us (58%)
  other arithmetic  67.5 us (13%)
  matrix products  64.5 us (13%)
  waiting for transfers between devices  47.7 us (9%)
  starting transfers between devices  26.9 us (5%)
    slice x2, local copies, waits for them, and re-layouts, lift_extended(): odd_part = lax.slice_in_dim(extended, 1, length, 2, dimension)  74.6 us
    slice x2, local copies, waits for them, and re-layouts, lift_extended(): even_part = lax.slice_in_dim(extended, 0, length, 2, dimension)  74.3 us
    unnamed x29, local copies, waits for them, and re-layouts  58.8 us
    dot_general x1, matrix products, local(): jnp.dot(stacked.reshape((-1, depth)), z_matrix, precision=lax.Precision.H...  43.5 us
    ppermute x4, waiting for transfers between devices, shifted(): return lax.ppermute(value, axis, pairs)  41.4 us
    transpose x1, local copies, waits for them, and re-layouts, local(): jnp.transpose(split, (0, 1, 3, 5, 2, 4, 6))  41.1 us
    sub x1, other arithmetic, local(): return (relaid, scaled - jnp.clip(scaled, -0.5, 0.5))  32.3 us
    dot_general x1, matrix products, local(): jnp.einsum('yk,abcyz->abckz', y_matrix, extended, precision=lax.Precision...  21.1 us
  transfers between devices with their start and end apart: 7, of which 5 were waited for; matrix products, arithmetic and copies ran while one was open for 46% of the time, Pallas kernels for 0%

commit v1 on v0

v1 whole, which is shorter than its diff:
```python
import functools

import jax
import jax.numpy as jnp
import ml_dtypes
import numpy as np
from jax import lax
from jax.experimental import pallas as pl
from jax.experimental.pallas import tpu as pltpu
from jax.sharding import PartitionSpec as P

MESH = pl.DeviceIdType.MESH
F32 = jnp.float32
BF16 = jnp.bfloat16

pa = -1.586134342
ub = -0.05298011854
pg = 0.8829110762
ue = 0.4435068522
scaling = 1.149604398

COMPS = 3
PLANES = 16
ROWS = 64
DEPTH = 1024
CHUNKS = DEPTH // 128
TILE = 256
WINDOW_START = (0, 128, 384, 512)
WINDOW_KIND = (0, 1, 1, 2)


def z_weights():
    ext = np.pad(np.eye(DEPTH), ((0, 0), (4, 4)), mode="reflect")
    s, d = ext[:, 0::2], ext[:, 1::2]
    d = d[:, :-1] + pa * (s[:, :-1] + s[:, 1:])
    s = s[:, 1:-1] + ub * (d[:, :-1] + d[:, 1:])
    d = d[:, 1:-1] + pg * (s[:, :-1] + s[:, 1:])
    s = s[:, 1:-1] + ue * (d[:, :-1] + d[:, 1:])
    low, high = s * scaling, d[:, 1:] / scaling
    kinds = []
    for k in (0, 1, 3):
        rows = slice(WINDOW_START[k], WINDOW_START[k] + 512)
        cols = slice(128 * k, 128 * k + 128)
        kinds.append(np.concatenate([low[rows, cols], high[rows, cols]], 1))
    full = np.stack(kinds)
    head = full.astype(np.float32).astype(ml_dtypes.bfloat16)
    rest = (full - head.astype(np.float64)).astype(np.float32).astype(ml_dtypes.bfloat16)
    return np.stack([head, rest], 1)


def kernel(
    n_narrow, n_wide,
    x_ref, e_ref, w_ref, ap_ref, det_ref,
    a_buf, b_buf, hl, wv, ys, yr, yz, xs, xr, lll, lsend, lrecv,
    load_sem, w_sem, y_send, y_recv, x_send, x_recv, l_send, l_recv,
):
    nar = lax.axis_index("narrow")
    wid = lax.axis_index("wide")
    up = lax.rem(nar + n_narrow - 1, n_narrow)
    down = lax.rem(nar + 1, n_narrow)
    left = lax.rem(wid + n_wide - 1, n_wide)
    right = lax.rem(wid + 1, n_wide)
    has_up, has_down = nar > 0, nar < n_narrow - 1
    has_left, has_right = wid > 0, wid < n_wide - 1

    def load(c, j):
        return pltpu.make_async_copy(
            x_ref.at[c, :, pl.ds(128 * j, 128)], a_buf.at[c, j], load_sem.at[c, j]
        )

    load_w = pltpu.make_async_copy(w_ref, wv, w_sem)
    for j in range(CHUNKS):
        load(0, j).start()
    load_w.start()
    for c in range(1, COMPS):
        for j in range(CHUNKS):
            load(c, j).start()

    barrier = pltpu.get_barrier_semaphore()

    def greet(off, carry):
        pl.semaphore_signal(
            barrier, inc=1, device_id={"wide": lax.rem(wid + off, n_wide)}, device_id_type=MESH
        )
        return carry

    lax.fori_loop(1, n_wide, greet, 0)

    @pl.when(has_up)
    def _():
        pl.semaphore_signal(barrier, inc=1, device_id={"narrow": up}, device_id_type=MESH)

    @pl.when(has_down)
    def _():
        pl.semaphore_signal(barrier, inc=1, device_id={"narrow": down}, device_id_type=MESH)

    pl.semaphore_wait(
        barrier, n_wide - 1 + has_up.astype(jnp.int32) + has_down.astype(jnp.int32)
    )

    def y_copy(side, c):
        return pltpu.make_async_remote_copy(
            src_ref=ys.at[side, c],
            dst_ref=yr.at[1 - side, c],
            send_sem=y_send.at[side, c],
            recv_sem=y_recv.at[1 - side, c],
            device_id={"narrow": up if side == 0 else down},
            device_id_type=MESH,
        )

    def y_values(c):
        for j in range(CHUNKS):
            load(c, j).wait()

        def body(j, carry):
            def row(r):
                return a_buf[c, j, pl.ds(r, PLANES, stride=ROWS), :]

            r0, r1, r2 = row(0), row(1), row(2)
            e0, e1, e2, e3 = row(ROWS - 4), row(ROWS - 3), row(ROWS - 2), row(ROWS - 1)
            before_last = e1 + pa * (e0 + e2)
            ys[0, c, j, 0:PLANES, :] = r0
            ys[0, c, j, PLANES:, :] = r1 + pa * (r0 + r2)
            ys[1, c, j, 0:PLANES, :] = e3 + pa * e2
            ys[1, c, j, PLANES:, :] = e2 + ub * before_last

            @pl.when(jnp.logical_not(has_up))
            def _():
                r3, r4 = row(3), row(4)
                yr[0, c, j, 0:PLANES, :] = r1 + pa * r2
                yr[0, c, j, PLANES:, :] = r2 + ub * (r3 + pa * (r2 + r4))

            @pl.when(jnp.logical_not(has_down))
            def _():
                yr[1, c, j, 0:PLANES, :] = e2
                yr[1, c, j, PLANES:, :] = before_last

            return carry

        lax.fori_loop(0, CHUNKS, body, 0)

        @pl.when(has_up)
        def _():
            y_copy(0, c).start()

        @pl.when(has_down)
        def _():
            y_copy(1, c).start()

    def z_rows(m, get, put):
        for j in range(CHUNKS):
            value = get(j)
            head = value.astype(BF16)
            hl[0:m, 128 * j : 128 * j + 128] = head
            hl[m : 2 * m, 128 * j : 128 * j + 128] = (value - head.astype(F32)).astype(BF16)
        for k in range(CHUNKS // 2):
            start, kind = WINDOW_START[k], WINDOW_KIND[k]
            both = jnp.dot(
                hl[0 : 2 * m, start : start + 512], wv[kind, 0], preferred_element_type=F32
            )
            rest = jnp.dot(hl[0:m, start : start + 512], wv[kind, 1], preferred_element_type=F32)
            out = both[:m] + (both[m:] + rest)
            put(k, out[:, :128])
            put(CHUNKS // 2 + k, out[:, 128:])

    def z_tiles(c, first, step):
        def body(t, carry):
            base = pl.multiple_of((first + step * t) * TILE, TILE)

            def put(j, value):
                b_buf[c, j, pl.ds(base, TILE), :] = value

            z_rows(TILE, lambda j: a_buf[c, j, pl.ds(base, TILE), :], put)
            return carry

        lax.fori_loop(0, 2, body, 0)

    def z_halo(c):
        @pl.when(has_up)
        def _():
            y_copy(1, c).wait_recv()

        @pl.when(has_down)
        def _():
            y_copy(0, c).wait_recv()

        def put(j, value):
            yz[c, j] = value

        z_rows(
            4 * PLANES,
            lambda j: jnp.concatenate([yr[0, c, j], yr[1, c, j]], 0),
            put,
        )

    half = ROWS // 2
    row_at = lax.broadcasted_iota(jnp.int32, (half, 128), 0)

    def following(value, last):
        return jnp.where(row_at == half - 1, last, pltpu.roll(value, half - 1, 0))

    def preceding(value, first):
        return jnp.where(row_at == 0, first, pltpu.roll(value, 1, 0))

    def y_plane(c, p, j):
        base = pl.multiple_of(p * ROWS, ROWS)
        s = b_buf[c, j, pl.ds(base, half, stride=2), :]
        d = b_buf[c, j, pl.ds(base + 1, half, stride=2), :]
        pv = yz[c, j, pl.ds(p, 1), :]
        qv = yz[c, j, pl.ds(PLANES + p, 1), :]
        sv = yz[c, j, pl.ds(2 * PLANES + p, 1), :]
        dv = yz[c, j, pl.ds(3 * PLANES + p, 1), :]
        d = d + pa * (s + following(s, sv))
        dm = pv + pa * s[0:1]
        s = s + ub * (preceding(d, dm) + d)
        sn = sv + ub * (d[half - 1 :] + dv)
        sm = qv + ub * dm
        dm = dm + pg * (sm + s[0:1])
        d = d + pg * (s + following(s, sn))
        s = s + ue * (preceding(d, dm) + d)
        a_buf[c, j, pl.ds(base, half), :] = s
        a_buf[c, j, pl.ds(base + half, half), :] = d

    def y_planes(c, starts):
        for start in starts:
            def body(q, carry):
                for j in range(CHUNKS):
                    y_plane(c, start + q, j)
                return carry

            lax.fori_loop(0, 4, body, 0)

    parts = ((0, 4, 0, half), (4, 4, 0, half), (0, 8, half, half))

    def x_copy(side, c, part):
        j0, jn, r0, rn = parts[part]
        place = (c, slice(None), pl.ds(j0, jn), pl.ds(r0, rn), slice(None))
        return pltpu.make_async_remote_copy(
            src_ref=xs.at[(side, *place)],
            dst_ref=xr.at[(1 - side, *place)],
            send_sem=x_send.at[side, c, part],
            recv_sem=x_recv.at[1 - side, c, part],
            device_id={"wide": left if side == 0 else right},
            device_id_type=MESH,
        )

    def x_values(c):
        def body(j, carry):
            def plane(p):
                return a_buf[c, j, p * ROWS : p * ROWS + ROWS, :]

            p0 = plane(0)
            xs[0, c, 0, j] = p0
            xs[0, c, 1, j] = plane(1) + pa * (p0 + plane(2))
            e2 = plane(PLANES - 2)
            xs[1, c, 0, j] = plane(PLANES - 1) + pa * e2
            xs[1, c, 1, j] = e2 + ub * (plane(PLANES - 3) + pa * (plane(PLANES - 4) + e2))
            return carry

        lax.fori_loop(0, CHUNKS, body, 0)

    def x_ends():
        def body(at, carry):
            c, j = at // CHUNKS, lax.rem(at, CHUNKS)

            def plane(p):
                return a_buf[c, j, p * ROWS : p * ROWS + ROWS, :]

            @pl.when(jnp.logical_not(has_left))
            def _():
                xr[0, c, 0, j] = plane(1) + pa * plane(2)
                xr[0, c, 1, j] = plane(2) + ub * (plane(3) + pa * (plane(2) + plane(4)))

            @pl.when(jnp.logical_not(has_right))
            def _():
                xr[1, c, 0, j] = plane(PLANES - 2)
                xr[1, c, 1, j] = plane(PLANES - 3) + pa * (plane(PLANES - 4) + plane(PLANES - 2))

            return carry

        lax.fori_loop(0, COMPS * CHUNKS, body, 0)

    def x_start(c, part):
        @pl.when(has_left)
        def _():
            x_copy(0, c, part).start()

        @pl.when(has_right)
        def _():
            x_copy(1, c, part).start()

    def x_arrived(c, part):
        @pl.when(has_left)
        def _():
            x_copy(1, c, part).wait_recv()

        @pl.when(has_right)
        def _():
            x_copy(0, c, part).wait_recv()

    def factor(band):
        shift = lax.shift_left(jnp.int32(1), 15 - e_ref[band - 1]).astype(F32)
        ups = 2 - 2 * (band // 4) - 2 * ((band // 2) % 2)
        return shift * (2.0**-15 * scaling**ups)

    def x_lift(c, by, bz):
        low_band, high_band = 2 * by + bz, 4 + 2 * by + bz
        high_scale = factor(high_band)
        low_scale = factor(low_band) if low_band else None

        def body(at, carry):
            k, t = at // 4, lax.rem(at, 4)
            j = 4 * bz + k
            row = pl.multiple_of(half * by + 8 * t, 8)

            def plane(p):
                return a_buf[c, j, pl.ds(pl.multiple_of(p * ROWS + row, 8), 8), :]

            s = [plane(2 * i) for i in range(8)]
            d = [plane(2 * i + 1) for i in range(8)]
            pv = xr[0, c, 0, j, pl.ds(row, 8), :]
            qv = xr[0, c, 1, j, pl.ds(row, 8), :]
            sv = xr[1, c, 0, j, pl.ds(row, 8), :]
            dv = xr[1, c, 1, j, pl.ds(row, 8), :]
            s.append(sv)
            d = [d[i] + pa * (s[i] + s[i + 1]) for i in range(8)]
            dm = pv + pa * s[0]
            sn = sv + ub * (d[7] + dv)
            sm = qv + ub * dm
            s = [s[i] + ub * ((d[i - 1] if i else dm) + d[i]) for i in range(8)]
            dm = dm + pg * (sm + s[0])
            s.append(sn)
            d = [d[i] + pg * (s[i] + s[i + 1]) for i in range(8)]
            s = [s[i] + ue * ((d[i - 1] if i else dm) + d[i]) for i in range(8)]
            lanes = pl.ds(pl.multiple_of(128 * k, 128), 128)
            rows = pl.ds(pl.multiple_of(8 * t, 8), 8)
            for i in range(8):
                v = d[i] * high_scale
                det_ref[c, high_band - 1, i, rows, lanes] = v - jnp.clip(v, -0.5, 0.5)
                if low_band:
                    v = s[i] * low_scale
                    det_ref[c, low_band - 1, i, rows, lanes] = v - jnp.clip(v, -0.5, 0.5)
                else:
                    lll[k, pl.ds(pl.multiple_of(half * i + 8 * t, 8), 8), :] = s[i] * (scaling * scaling)
            return carry

        lax.fori_loop(0, 16, body, 0)

    lane = lax.broadcasted_iota(jnp.int32, (8, 128), 1)
    low_half = lane < 64
    low_quarter = lax.rem(lane, 64) < 32

    def l_copy(c, peer, source):
        return pltpu.make_async_remote_copy(
            src_ref=lsend.at[peer, c],
            dst_ref=lrecv.at[c, :, pl.ds(pl.multiple_of(source * 8, 8), 8), :],
            send_sem=l_send.at[c, peer],
            recv_sem=l_recv.at[c, source],
            device_id={"wide": peer},
            device_id_type=MESH,
        )

    def l_pack(c):
        def body(at, carry):
            k, g = at // 8, lax.rem(at, 8)
            v = [lll[k, pl.ds(4 * g + y, 8, stride=half), :] for y in range(4)]
            for a, b in ((0, 2), (1, 3)):
                v[a], v[b] = (
                    jnp.where(low_half, v[a], pltpu.roll(v[b], 64, 1)),
                    jnp.where(low_half, pltpu.roll(v[a], 64, 1), v[b]),
                )
            for a, b in ((0, 1), (2, 3)):
                v[a], v[b] = (
                    jnp.where(low_quarter, v[a], pltpu.roll(v[b], 32, 1)),
                    jnp.where(low_quarter, pltpu.roll(v[a], 96, 1), v[b]),
                )
            for y in range(4):
                lsend[4 * k + y, c, g] = v[y]
            return carry

        lax.fori_loop(0, 32, body, 0)

        def send(off, carry):
            l_copy(c, lax.rem(wid + off, n_wide), wid).start()
            return carry

        lax.fori_loop(1, n_wide, send, 0)
        lrecv[c, :, pl.ds(pl.multiple_of(wid * 8, 8), 8), :] = lsend[wid, c]

    def l_take(c):
        def arrived(off, carry):
            source = lax.rem(wid + off, n_wide)
            l_copy(c, source, source).wait_recv()
            return carry

        lax.fori_loop(1, n_wide, arrived, 0)

        def body(g, carry):
            ap_ref[c, pl.ds(pl.multiple_of(128 * g, 128), 128), :] = lrecv[c, g].T
            return carry

        lax.fori_loop(0, 8, body, 0)

    y_values(0)
    load_w.wait()
    z_tiles(0, 0, 3)
    y_values(1)
    y_values(2)
    for c in range(COMPS):
        if c:
            z_tiles(c, 0, 3)
        z_halo(c)
        y_planes(c, (0, 12))
        x_values(c)
        x_start(c, 0)
        x_start(c, 1)
    for c in range(COMPS):
        x_start(c, 2)
    for c in range(COMPS):
        z_tiles(c, 1, 1)
        y_planes(c, (4, 8))
    x_ends()
    for c in range(COMPS):
        x_arrived(c, 0)
        x_lift(c, 0, 0)
        l_pack(c)
        x_arrived(c, 1)
        x_lift(c, 0, 1)
    for c in range(COMPS):
        x_arrived(c, 2)
        x_lift(c, 1, 0)
        x_lift(c, 1, 1)
        l_take(c)

    for c in range(COMPS):
        @pl.when(has_up)
        def _():
            y_copy(0, c).wait_send()

        @pl.when(has_down)
        def _():
            y_copy(1, c).wait_send()

        for part in range(3):
            @pl.when(has_left)
            def _():
                x_copy(0, c, part).wait_send()

            @pl.when(has_right)
            def _():
                x_copy(1, c, part).wait_send()

        def sent(off, carry):
            peer = lax.rem(wid + off, n_wide)
            l_copy(c, peer, wid).wait_send()
            return carry

        lax.fori_loop(1, n_wide, sent, 0)


def local(n_narrow, n_wide, velocity, exponents):
    cells = velocity.reshape((COMPS, PLANES * ROWS, DEPTH))
    approx, details = pl.pallas_call(
        functools.partial(kernel, n_narrow, n_wide),
        out_shape=(
            jax.ShapeDtypeStruct((COMPS, 1024, 128), F32),
            jax.ShapeDtypeStruct((COMPS, 7, PLANES // 2, ROWS // 2, DEPTH // 2), F32),
        ),
        in_specs=[
            pl.BlockSpec(memory_space=pl.ANY),
            pl.BlockSpec(memory_space=pltpu.SMEM),
            pl.BlockSpec(memory_space=pl.ANY),
        ],
        out_specs=(
            pl.BlockSpec(memory_space=pltpu.VMEM),
            pl.BlockSpec(memory_space=pltpu.VMEM),
        ),
        scratch_shapes=[
            pltpu.VMEM((COMPS, CHUNKS, PLANES * ROWS, 128), F32),
            pltpu.VMEM((COMPS, CHUNKS, PLANES * ROWS, 128), F32),
            pltpu.VMEM((2 * TILE, DEPTH), BF16),
            pltpu.VMEM((3, 2, 512, 256), BF16),
            pltpu.VMEM((2, COMPS, CHUNKS, 2 * PLANES, 128), F32),
            pltpu.VMEM((2, COMPS, CHUNKS, 2 * PLANES, 128), F32),
            pltpu.VMEM((COMPS, CHUNKS, 4 * PLANES, 128), F32),
            pltpu.VMEM((2, COMPS, 2, CHUNKS, ROWS, 128), F32),
            pltpu.VMEM((2, COMPS, 2, CHUNKS, ROWS, 128), F32),
            pltpu.VMEM((4, 256, 128), F32),
            pltpu.VMEM((16, COMPS, 8, 8, 128), F32),
            pltpu.VMEM((COMPS, 8, 128, 128), F32),
            pltpu.SemaphoreType.DMA((COMPS, CHUNKS)),
            pltpu.SemaphoreType.DMA,
            pltpu.SemaphoreType.DMA((2, COMPS)),
            pltpu.SemaphoreType.DMA((2, COMPS)),
            pltpu.SemaphoreType.DMA((2, COMPS, 3)),
            pltpu.SemaphoreType.DMA((2, COMPS, 3)),
            pltpu.SemaphoreType.DMA((COMPS, 16)),
            pltpu.SemaphoreType.DMA((COMPS, 16)),
        ],
        compiler_params=pltpu.CompilerParams(
            collective_id=0, has_side_effects=True, vmem_limit_bytes=60 * 1024 * 1024
        ),
        cost_estimate=pl.CostEstimate(
            flops=10_000_000_000, bytes_accessed=26_000_000, transcendentals=0
        ),
    )(cells, exponents, jnp.asarray(z_weights()))
    approx = approx.reshape((COMPS, ROWS // 2, 32, 128))
    return jnp.transpose(approx, (0, 3, 1, 2)), details


def solution(mesh):
    placed = (P(None, "wide", "narrow", None), P())
    return jax.shard_map(
        functools.partial(local, mesh.shape["narrow"], mesh.shape["wide"]),
        mesh=mesh,
        in_specs=placed,
        out_specs=(P(None, None, "narrow", "wide"), P(None, None, "wide", "narrow", None)),
        check_vma=False,
    )
```

time: 515 us -> 99.4 us (0.19); the launches traced: 505 us -> 99 us
  local copies, waits for them, and re-layouts: 297 us -> 13.6 us
  Pallas kernels: 0 us -> 84.7 us
  other arithmetic: 67.5 us -> 0 us
  matrix products: 64.5 us -> 0 us
  waiting for transfers between devices: 47.7 us -> 0 us
  starting transfers between devices: 26.9 us -> 0 us
    slice x16 -> x0, local copies, waits for them, and re-layouts: 163 us -> none  [the longest x2 74.6 us: lift_extended(): odd_part = lax.slice_in_dim(extended, 1, length, 2, dimension)]
    pallas_call x0 -> x1, Pallas kernels: none -> 84.7 us  [local(): pl.pallas_call(functools.partial(kernel, n_narrow, n_wide), out_shape=(ja...]
    dot_general x2 -> x0, matrix products: 64.5 us -> none  [the longest x1 43.5 us: local(): jnp.dot(stacked.reshape((-1, depth)), z_matrix, precision=lax.Precision.H...]
    ppermute x6 -> x0, waiting for transfers between devices: 47.7 us -> none  [the longest x4 41.4 us: shifted(): return lax.ppermute(value, axis, pairs)]
    unnamed x29 -> x2, local copies, waits for them, and re-layouts: 58.8 us -> 13.6 us
    transpose x1 -> x0, local copies, waits for them, and re-layouts: 41.1 us -> none  [local(): jnp.transpose(split, (0, 1, 3, 5, 2, 4, 6))]
    sub x1 -> x0, other arithmetic: 32.3 us -> none  [local(): return (relaid, scaled - jnp.clip(scaled, -0.5, 0.5))]
    ppermute x6 -> x0, starting transfers between devices: 17.6 us -> none  [the longest x4 12.3 us: shifted(): return lax.ppermute(value, axis, pairs)]
  transfers between devices with their start and end apart: 7 -> 0, of which waited for: 5 -> 0; matrix products, arithmetic and copies ran while one was open for 46% -> 0% of each run, Pallas kernels for 0% -> 0%
where the time goes in v1:
time: 99.4 us; the launch traced here: 99 us
  Pallas kernels  84.7 us (85%)
  local copies, waits for them, and re-layouts  13.6 us (14%)
    pallas_call x1, Pallas kernels, local(): pl.pallas_call(functools.partial(kernel, n_narrow, n_wide), out_shape=(ja...  84.7 us
    unnamed x2, local copies, waits for them, and re-layouts  13.6 us

profile of v1, /device:TPU:24, one launch (start us, length us, event | category | flops | bytes accessed | tf_op | source)
XLA Modules:
  0.0 99.0 jit_solution(14256029597940100537)
XLA Ops:
  0.6 84.7 %shard_map.50 = (f32[3,1024,128]{2,1,0:T(8,128)}, f32[3,7,8,32,512]{4,3,2,1,0:T(8,128)}) custom-call(f32[3,1024,1024]{2,1,0:T(8,128)} %bitcast.5, s32[7]{0:T(128)} %e_ref.1, bf16[3,2,512,256]{3,2,1,0:T(8,128)(2,1)} %constant.2.clone.w_ref), custom_call_target="tpu_custom_call" | custom-call | flops 10000000000 | bytes 26000000 | tf_op jit(solution)/shard_map/pallas_call | solution.py:463
  85.4 2.7 %copy.7 = f32[3,128,32,32]{1,3,2,0:T(8,128)} copy(f32[3,128,32,32]{1,3,2,0:T(8,128)} %bitcast.4) | data formatting | bytes 3145728
  88.0 10.9 %copy.8 = f32[3,7,8,32,512]{4,3,2,1,0:T(8,128)} copy(f32[3,7,8,32,512]{4,3,2,1,0:T(8,128)} %get-tuple-element.9) | data formatting | bytes 22020096

commit v2 on v1

--- a/solution.py
+++ b/solution.py
@@ -51,7 +51,7 @@
 def kernel(
     n_narrow, n_wide,
     x_ref, e_ref, w_ref, ap_ref, det_ref,
-    a_buf, b_buf, hl, wv, ys, yr, yz, xs, xr, lll, lsend, lrecv,
+    a_buf, b_buf, hl, wv, ys, yr, yz, xs, xr, lll, lsend, lmid, lrecv,
     load_sem, w_sem, y_send, y_recv, x_send, x_recv, l_send, l_recv,
 ):
     nar = lax.axis_index("narrow")
@@ -72,9 +72,6 @@
     for j in range(CHUNKS):
         load(0, j).start()
     load_w.start()
-    for c in range(1, COMPS):
-        for j in range(CHUNKS):
-            load(c, j).start()
 
     barrier = pltpu.get_barrier_semaphore()
 
@@ -111,6 +108,9 @@
     def y_values(c):
         for j in range(CHUNKS):
             load(c, j).wait()
+        if c + 1 < COMPS:
+            for j in range(CHUNKS):
+                load(c + 1, j).start()
 
         def body(j, carry):
             def row(r):
@@ -259,9 +259,8 @@
 
         lax.fori_loop(0, CHUNKS, body, 0)
 
-    def x_ends():
-        def body(at, carry):
-            c, j = at // CHUNKS, lax.rem(at, CHUNKS)
+    def x_ends(c):
+        def body(j, carry):
 
             def plane(p):
                 return a_buf[c, j, p * ROWS : p * ROWS + ROWS, :]
@@ -278,7 +277,7 @@
 
             return carry
 
-        lax.fori_loop(0, COMPS * CHUNKS, body, 0)
+        lax.fori_loop(0, CHUNKS, body, 0)
 
     def x_start(c, part):
         @pl.when(has_left)
@@ -350,53 +349,73 @@
     low_half = lane < 64
     low_quarter = lax.rem(lane, 64) < 32
 
-    def l_copy(c, peer, source):
+    xpos, zpos = wid // 4, lax.rem(wid, 4)
+
+    def across(c, off, source):
+        peer = lax.rem(xpos + off, 4)
         return pltpu.make_async_remote_copy(
-            src_ref=lsend.at[peer, c],
-            dst_ref=lrecv.at[c, :, pl.ds(pl.multiple_of(source * 8, 8), 8), :],
-            send_sem=l_send.at[c, peer],
-            recv_sem=l_recv.at[c, source],
-            device_id={"wide": peer},
+            src_ref=lsend.at[pl.ds(4 * peer, 4), c],
+            dst_ref=lmid.at[c, :, :, source],
+            send_sem=l_send.at[0, c, off - 1],
+            recv_sem=l_recv.at[0, c, source],
+            device_id={"wide": 4 * peer + zpos},
             device_id_type=MESH,
         )
 
+    def along(c, off, source):
+        peer = lax.rem(zpos + off, 4)
+        return pltpu.make_async_remote_copy(
+            src_ref=lmid.at[c, peer],
+            dst_ref=lrecv.at[c, :, :, source],
+            send_sem=l_send.at[1, c, off - 1],
+            recv_sem=l_recv.at[1, c, source],
+            device_id={"wide": 4 * xpos + peer},
+            device_id_type=MESH,
+        )
+
     def l_pack(c):
-        def body(at, carry):
-            k, g = at // 8, lax.rem(at, 8)
-            v = [lll[k, pl.ds(4 * g + y, 8, stride=half), :] for y in range(4)]
-            for a, b in ((0, 2), (1, 3)):
-                v[a], v[b] = (
-                    jnp.where(low_half, v[a], pltpu.roll(v[b], 64, 1)),
-                    jnp.where(low_half, pltpu.roll(v[a], 64, 1), v[b]),
-                )
-            for a, b in ((0, 1), (2, 3)):
-                v[a], v[b] = (
-                    jnp.where(low_quarter, v[a], pltpu.roll(v[b], 32, 1)),
-                    jnp.where(low_quarter, pltpu.roll(v[a], 96, 1), v[b]),
-                )
-            for y in range(4):
-                lsend[4 * k + y, c, g] = v[y]
-            return carry
-
-        lax.fori_loop(0, 32, body, 0)
-
-        def send(off, carry):
-            l_copy(c, lax.rem(wid + off, n_wide), wid).start()
-            return carry
-
-        lax.fori_loop(1, n_wide, send, 0)
-        lrecv[c, :, pl.ds(pl.multiple_of(wid * 8, 8), 8), :] = lsend[wid, c]
+        def body(k, carry):
+            for g in range(8):
+                v = [lll[k, pl.ds(4 * g + y, 8, stride=half), :] for y in range(4)]
+                for a, b in ((0, 2), (1, 3)):
+                    v[a], v[b] = (
+                        jnp.where(low_half, v[a], pltpu.roll(v[b], 64, 1)),
+                        jnp.where(low_half, pltpu.roll(v[a], 64, 1), v[b]),
+                    )
+                for a, b in ((0, 1), (2, 3)):
+                    v[a], v[b] = (
+                        jnp.where(low_quarter, v[a], pltpu.roll(v[b], 32, 1)),
+                        jnp.where(low_quarter, pltpu.roll(v[a], 96, 1), v[b]),
+                    )
+                for y in range(4):
+                    lsend[4 * k + y, c, g] = v[y]
+            return carry
+
+        lax.fori_loop(0, 4, body, 0)
+
+        for off in (2, 1, 3):
+            across(c, off, xpos).start()
+
+        def own(z, carry):
+            lmid[c, z, :, xpos] = lsend[4 * xpos + z, c]
+            return carry
+
+        lax.fori_loop(0, 4, own, 0)
+
+    def l_turn(c):
+        for off in (2, 1, 3):
+            across(c, off, lax.rem(xpos + off, 4)).wait_recv()
+        for off in (2, 1, 3):
+            along(c, off, zpos).start()
+        lrecv[c, :, :, zpos] = lmid[c, zpos]
 
     def l_take(c):
-        def arrived(off, carry):
-            source = lax.rem(wid + off, n_wide)
-            l_copy(c, source, source).wait_recv()
-            return carry
-
-        lax.fori_loop(1, n_wide, arrived, 0)
+        for off in (2, 1, 3):
+            along(c, off, lax.rem(zpos + off, 4)).wait_recv()
 
         def body(g, carry):
-            ap_ref[c, pl.ds(pl.multiple_of(128 * g, 128), 128), :] = lrecv[c, g].T
+            block = lrecv[c, g].reshape((128, 128))
+            ap_ref[c, pl.ds(pl.multiple_of(128 * g, 128), 128), :] = block.T
             return carry
 
         lax.fori_loop(0, 8, body, 0)
@@ -414,18 +433,36 @@
         x_values(c)
         x_start(c, 0)
         x_start(c, 1)
-    for c in range(COMPS):
-        x_start(c, 2)
-    for c in range(COMPS):
-        z_tiles(c, 1, 1)
-        y_planes(c, (4, 8))
-    x_ends()
-    for c in range(COMPS):
-        x_arrived(c, 0)
-        x_lift(c, 0, 0)
-        l_pack(c)
-        x_arrived(c, 1)
-        x_lift(c, 0, 1)
+    x_start(0, 2)
+    z_tiles(0, 1, 1)
+    y_planes(0, (4, 8))
+    x_ends(0)
+    x_arrived(0, 0)
+    x_lift(0, 0, 0)
+    l_pack(0)
+    z_tiles(1, 1, 1)
+    y_planes(1, (4, 8))
+    x_ends(1)
+    x_arrived(1, 0)
+    x_lift(1, 0, 0)
+    l_pack(1)
+    l_turn(0)
+    x_start(1, 2)
+    z_tiles(2, 1, 1)
+    y_planes(2, (4, 8))
+    x_ends(2)
+    x_arrived(2, 0)
+    x_lift(2, 0, 0)
+    l_pack(2)
+    l_turn(1)
+    x_start(2, 2)
+    x_arrived(0, 1)
+    x_lift(0, 0, 1)
+    l_turn(2)
+    x_arrived(1, 1)
+    x_lift(1, 0, 1)
+    x_arrived(2, 1)
+    x_lift(2, 0, 1)
     for c in range(COMPS):
         x_arrived(c, 2)
         x_lift(c, 1, 0)
@@ -450,12 +487,9 @@
             def _():
                 x_copy(1, c, part).wait_send()
 
-        def sent(off, carry):
-            peer = lax.rem(wid + off, n_wide)
-            l_copy(c, peer, wid).wait_send()
-            return carry
-
-        lax.fori_loop(1, n_wide, sent, 0)
+        for off in (1, 2, 3):
+            across(c, off, xpos).wait_send()
+            along(c, off, zpos).wait_send()
 
 
 def local(n_narrow, n_wide, velocity, exponents):
@@ -463,8 +497,8 @@
     approx, details = pl.pallas_call(
         functools.partial(kernel, n_narrow, n_wide),
         out_shape=(
-            jax.ShapeDtypeStruct((COMPS, 1024, 128), F32),
-            jax.ShapeDtypeStruct((COMPS, 7, PLANES // 2, ROWS // 2, DEPTH // 2), F32),
+            pltpu.VMEM((COMPS, 1024, 128), F32),
+            pltpu.VMEM((COMPS, 7, PLANES // 2, ROWS // 2, DEPTH // 2), F32),
         ),
         in_specs=[
             pl.BlockSpec(memory_space=pl.ANY),
@@ -487,18 +521,19 @@
             pltpu.VMEM((2, COMPS, 2, CHUNKS, ROWS, 128), F32),
             pltpu.VMEM((4, 256, 128), F32),
             pltpu.VMEM((16, COMPS, 8, 8, 128), F32),
-            pltpu.VMEM((COMPS, 8, 128, 128), F32),
+            pltpu.VMEM((COMPS, 4, 8, 4, 8, 128), F32),
+            pltpu.VMEM((COMPS, 8, 4, 4, 8, 128), F32),
             pltpu.SemaphoreType.DMA((COMPS, CHUNKS)),
             pltpu.SemaphoreType.DMA,
             pltpu.SemaphoreType.DMA((2, COMPS)),
             pltpu.SemaphoreType.DMA((2, COMPS)),
             pltpu.SemaphoreType.DMA((2, COMPS, 3)),
             pltpu.SemaphoreType.DMA((2, COMPS, 3)),
-            pltpu.SemaphoreType.DMA((COMPS, 16)),
-            pltpu.SemaphoreType.DMA((COMPS, 16)),
+            pltpu.SemaphoreType.DMA((2, COMPS, 3)),
+            pltpu.SemaphoreType.DMA((2, COMPS, 4)),
         ],
         compiler_params=pltpu.CompilerParams(
-            collective_id=0, has_side_effects=True, vmem_limit_bytes=60 * 1024 * 1024
+            collective_id=0, has_side_effects=True, vmem_limit_bytes=48 * 1024 * 1024
         ),
         cost_estimate=pl.CostEstimate(
             flops=10_000_000_000, bytes_accessed=26_000_000, transcendentals=0

time: 99.4 us -> 80.4 us (0.81)
  the two profiles are of different devices: /device:TPU:24 before, /device:TPU:11 now
where the time goes in v2:
time: 80.4 us; the launch traced here: 80.3 us
  Pallas kernels  74.3 us (92%)
  local copies, waits for them, and re-layouts  5.4 us (7%)
    pallas_call x1, Pallas kernels, local(): pl.pallas_call(functools.partial(kernel, n_narrow, n_wide), out_shape=(pl...  74.3 us
    unnamed x2, local copies, waits for them, and re-layouts  5.4 us

profile of v2, /device:TPU:11, one launch (start us, length us, event | category | flops | bytes accessed | tf_op | source)
XLA Modules:
  0.0 80.3 jit_solution(9996781598554606602)
XLA Ops:
  0.6 74.3 %shard_map.50 = (f32[3,1024,128]{2,1,0:T(8,128)S(1)}, f32[3,7,8,32,512]{4,3,2,1,0:T(8,128)S(1)}) custom-call(f32[3,1024,1024]{2,1,0:T(8,128)} %bitcast.5, s32[7]{0:T(128)} %e_ref.1, bf16[3,2,512,256]{3,2,1,0:T(8,128)(2,1)} %constant.2.clone.w_ref), custom_call_target="tpu_custom_call" | custom-call | flops 10000000000 | bytes 26000000 | tf_op jit(solution)/shard_map/pallas_call | solution.py:497
  74.9 1.1 %copy.7 = f32[3,128,32,32]{1,3,2,0:T(8,128)} copy(f32[3,128,32,32]{1,3,2,0:T(8,128)S(1)} %bitcast.4) | data formatting | bytes 3145728
  76.1 4.3 %copy.8 = f32[3,7,8,32,512]{4,3,2,1,0:T(8,128)} copy(f32[3,7,8,32,512]{4,3,2,1,0:T(8,128)S(1)} %get-tuple-element.7) | data formatting | bytes 22020096

commit v3 on v2

--- a/solution.py
+++ b/solution.py
@@ -51,8 +51,8 @@
 def kernel(
     n_narrow, n_wide,
     x_ref, e_ref, w_ref, ap_ref, det_ref,
-    a_buf, b_buf, hl, wv, ys, yr, yz, xs, xr, lll, lsend, lmid, lrecv,
-    load_sem, w_sem, y_send, y_recv, x_send, x_recv, l_send, l_recv,
+    a_buf, b_buf, hl, wv, ys, yr, yz, xs, xr, ms, mr, lll, lsend, lmid, lrecv,
+    load_sem, w_sem, y_send, y_recv, x_send, x_recv, m_send, m_recv, l_send, l_recv,
 ):
     nar = lax.axis_index("narrow")
     wid = lax.axis_index("wide")
@@ -105,13 +105,14 @@
             device_id_type=MESH,
         )
 
-    def y_values(c):
+    def loaded(c):
         for j in range(CHUNKS):
             load(c, j).wait()
         if c + 1 < COMPS:
             for j in range(CHUNKS):
                 load(c + 1, j).start()
 
+    def y_values(c):
         def body(j, carry):
             def row(r):
                 return a_buf[c, j, pl.ds(r, PLANES, stride=ROWS), :]
@@ -163,7 +164,7 @@
             put(k, out[:, :128])
             put(CHUNKS // 2 + k, out[:, 128:])
 
-    def z_tiles(c, first, step):
+    def z_tiles(c, first, step, count=2):
         def body(t, carry):
             base = pl.multiple_of((first + step * t) * TILE, TILE)
 
@@ -173,17 +174,18 @@
             z_rows(TILE, lambda j: a_buf[c, j, pl.ds(base, TILE), :], put)
             return carry
 
-        lax.fori_loop(0, 2, body, 0)
+        lax.fori_loop(0, count, body, 0)
+
+    def y_arrived(c):
+        @pl.when(has_up)
+        def _():
+            y_copy(1, c).wait_recv()
+
+        @pl.when(has_down)
+        def _():
+            y_copy(0, c).wait_recv()
 
     def z_halo(c):
-        @pl.when(has_up)
-        def _():
-            y_copy(1, c).wait_recv()
-
-        @pl.when(has_down)
-        def _():
-            y_copy(0, c).wait_recv()
-
         def put(j, value):
             yz[c, j] = value
 
@@ -204,12 +206,14 @@
 
     def y_plane(c, p, j):
         base = pl.multiple_of(p * ROWS, ROWS)
+        s, d = y_rows(c, j, base, [yz[c, j, pl.ds(PLANES * kind + p, 1), :] for kind in range(4)])
+        a_buf[c, j, pl.ds(base, half), :] = s
+        a_buf[c, j, pl.ds(base + half, half), :] = d
+
+    def y_rows(c, j, base, rim):
         s = b_buf[c, j, pl.ds(base, half, stride=2), :]
         d = b_buf[c, j, pl.ds(base + 1, half, stride=2), :]
-        pv = yz[c, j, pl.ds(p, 1), :]
-        qv = yz[c, j, pl.ds(PLANES + p, 1), :]
-        sv = yz[c, j, pl.ds(2 * PLANES + p, 1), :]
-        dv = yz[c, j, pl.ds(3 * PLANES + p, 1), :]
+        pv, qv, sv, dv = rim
         d = d + pa * (s + following(s, sv))
         dm = pv + pa * s[0:1]
         s = s + ub * (preceding(d, dm) + d)
@@ -218,8 +222,7 @@
         dm = dm + pg * (sm + s[0:1])
         d = d + pg * (s + following(s, sn))
         s = s + ue * (preceding(d, dm) + d)
-        a_buf[c, j, pl.ds(base, half), :] = s
-        a_buf[c, j, pl.ds(base + half, half), :] = d
+        return s, d
 
     def y_planes(c, starts):
         for start in starts:
@@ -230,7 +233,7 @@
 
             lax.fori_loop(0, 4, body, 0)
 
-    parts = ((0, 4, 0, half), (4, 4, 0, half), (0, 8, half, half))
+    parts = ((0, 4, 0, half), (4, 4, 0, half), (0, 8, half, half), (0, 8, 0, ROWS))
 
     def x_copy(side, c, part):
         j0, jn, r0, rn = parts[part]
@@ -296,6 +299,84 @@
         @pl.when(has_right)
         def _():
             x_copy(0, c, part).wait_recv()
+
+    def m_copy(side):
+        return pltpu.make_async_remote_copy(
+            src_ref=ms.at[side],
+            dst_ref=mr.at[1 - side],
+            send_sem=m_send.at[side],
+            recv_sem=m_recv.at[1 - side],
+            device_id={"wide": left if side == 0 else right},
+            device_id_type=MESH,
+        )
+
+    def m_values():
+        def body(j, carry):
+            for kind in range(4):
+                def row(p):
+                    return yr[kind // 2, 0, j, pl.ds(PLANES * (kind % 2) + p, 1), :]
+
+                e2 = row(PLANES - 2)
+                ms[0, j, kind : kind + 1, :] = row(0)
+                ms[0, j, 4 + kind : 5 + kind, :] = row(1) + pa * (row(0) + row(2))
+                ms[1, j, kind : kind + 1, :] = row(PLANES - 1) + pa * e2
+                ms[1, j, 4 + kind : 5 + kind, :] = e2 + ub * (
+                    row(PLANES - 3) + pa * (row(PLANES - 4) + e2)
+                )
+            return carry
+
+        lax.fori_loop(0, CHUNKS, body, 0)
+
+        @pl.when(has_left)
+        def _():
+            m_copy(0).start()
+
+        @pl.when(has_right)
+        def _():
+            m_copy(1).start()
+
+    def m_lift():
+        x_arrived(0, 3)
+
+        @pl.when(has_left)
+        def _():
+            m_copy(1).wait_recv()
+
+        @pl.when(has_right)
+        def _():
+            m_copy(0).wait_recv()
+
+        def get(j):
+            return jnp.concatenate(
+                [xr[0, 0, 0, j], xr[0, 0, 1, j], xr[1, 0, 0, j], xr[1, 0, 1, j], mr[0, j], mr[1, j]], 0
+            )
+
+        def put(j, value):
+            b_buf[0, j, 0 : TILE + 16, :] = value
+
+        z_rows(TILE + 16, get, put)
+
+        def side_lift(side):
+            def body(j, carry):
+                for combo in range(2):
+                    at = TILE + 8 * side + 4 * combo
+                    s, d = y_rows(
+                        0, j, ROWS * (2 * side + combo),
+                        [b_buf[0, j, at + kind : at + kind + 1, :] for kind in range(4)],
+                    )
+                    xr[side, 0, combo, j, 0:half, :] = s
+                    xr[side, 0, combo, j, half:, :] = d
+                return carry
+
+            lax.fori_loop(0, CHUNKS, body, 0)
+
+        @pl.when(has_left)
+        def _():
+            side_lift(0)
+
+        @pl.when(has_right)
+        def _():
+            side_lift(1)
 
     def factor(band):
         shift = lax.shift_left(jnp.int32(1), 15 - e_ref[band - 1]).astype(F32)
@@ -420,54 +501,70 @@
 
         lax.fori_loop(0, 8, body, 0)
 
+    loaded(0)
+    x_values(0)
+    x_start(0, 3)
+    loaded(1)
+    y_values(1)
     y_values(0)
     load_w.wait()
-    z_tiles(0, 0, 3)
-    y_values(1)
+    z_tiles(1, 0, 3)
+    loaded(2)
     y_values(2)
-    for c in range(COMPS):
-        if c:
-            z_tiles(c, 0, 3)
-        z_halo(c)
-        y_planes(c, (0, 12))
-        x_values(c)
-        x_start(c, 0)
-        x_start(c, 1)
-    x_start(0, 2)
-    z_tiles(0, 1, 1)
-    y_planes(0, (4, 8))
+    y_arrived(1)
+    z_halo(1)
+    y_planes(1, (0, 12))
+    x_values(1)
+    x_start(1, 0)
+    x_start(1, 1)
+    y_arrived(0)
+    m_values()
+    z_tiles(2, 0, 3)
+    y_arrived(2)
+    z_halo(2)
+    y_planes(2, (0, 12))
+    x_values(2)
+    x_start(2, 0)
+    x_start(2, 1)
+    z_tiles(0, 0, 1, 4)
+    z_halo(0)
+    y_planes(0, (0, 4, 8, 12))
+    m_lift()
     x_ends(0)
-    x_arrived(0, 0)
     x_lift(0, 0, 0)
     l_pack(0)
+    x_start(1, 2)
+    x_lift(0, 0, 1)
     z_tiles(1, 1, 1)
     y_planes(1, (4, 8))
+    l_turn(0)
     x_ends(1)
     x_arrived(1, 0)
     x_lift(1, 0, 0)
     l_pack(1)
-    l_turn(0)
-    x_start(1, 2)
     z_tiles(2, 1, 1)
     y_planes(2, (4, 8))
+    l_turn(1)
+    x_start(2, 2)
     x_ends(2)
     x_arrived(2, 0)
     x_lift(2, 0, 0)
     l_pack(2)
-    l_turn(1)
-    x_start(2, 2)
-    x_arrived(0, 1)
-    x_lift(0, 0, 1)
+    x_lift(0, 1, 0)
     l_turn(2)
-    x_arrived(1, 1)
-    x_lift(1, 0, 1)
-    x_arrived(2, 1)
-    x_lift(2, 0, 1)
-    for c in range(COMPS):
-        x_arrived(c, 2)
-        x_lift(c, 1, 0)
-        x_lift(c, 1, 1)
-        l_take(c)
+    x_lift(0, 1, 1)
+    for c in (1, 2):
+        x_arrived(c, 1)
+        x_lift(c, 0, 1)
+    x_arrived(1, 2)
+    x_lift(1, 1, 0)
+    x_lift(1, 1, 1)
+    l_take(0)
+    l_take(1)
+    x_arrived(2, 2)
+    x_lift(2, 1, 0)
+    x_lift(2, 1, 1)
+    l_take(2)
 
     for c in range(COMPS):
         @pl.when(has_up)
@@ -478,7 +575,7 @@
         def _():
             y_copy(1, c).wait_send()
 
-        for part in range(3):
+        for part in (range(3) if c else (3,)):
             @pl.when(has_left)
             def _():
                 x_copy(0, c, part).wait_send()
@@ -486,6 +583,15 @@
             @pl.when(has_right)
             def _():
                 x_copy(1, c, part).wait_send()
+
+        if c == 0:
+            @pl.when(has_left)
+            def _():
+                m_copy(0).wait_send()
+
+            @pl.when(has_right)
+            def _():
+                m_copy(1).wait_send()
 
         for off in (1, 2, 3):
             across(c, off, xpos).wait_send()
@@ -512,13 +618,15 @@
         scratch_shapes=[
             pltpu.VMEM((COMPS, CHUNKS, PLANES * ROWS, 128), F32),
             pltpu.VMEM((COMPS, CHUNKS, PLANES * ROWS, 128), F32),
-            pltpu.VMEM((2 * TILE, DEPTH), BF16),
+            pltpu.VMEM((2 * TILE + 32, DEPTH), BF16),
             pltpu.VMEM((3, 2, 512, 256), BF16),
             pltpu.VMEM((2, COMPS, CHUNKS, 2 * PLANES, 128), F32),
             pltpu.VMEM((2, COMPS, CHUNKS, 2 * PLANES, 128), F32),
             pltpu.VMEM((COMPS, CHUNKS, 4 * PLANES, 128), F32),
             pltpu.VMEM((2, COMPS, 2, CHUNKS, ROWS, 128), F32),
             pltpu.VMEM((2, COMPS, 2, CHUNKS, ROWS, 128), F32),
+            pltpu.VMEM((2, CHUNKS, 8, 128), F32),
+            pltpu.VMEM((2, CHUNKS, 8, 128), F32),
             pltpu.VMEM((4, 256, 128), F32),
             pltpu.VMEM((16, COMPS, 8, 8, 128), F32),
             pltpu.VMEM((COMPS, 4, 8, 4, 8, 128), F32),
@@ -527,8 +635,10 @@
             pltpu.SemaphoreType.DMA,
             pltpu.SemaphoreType.DMA((2, COMPS)),
             pltpu.SemaphoreType.DMA((2, COMPS)),
-            pltpu.SemaphoreType.DMA((2, COMPS, 3)),
-            pltpu.SemaphoreType.DMA((2, COMPS, 3)),
+            pltpu.SemaphoreType.DMA((2, COMPS, 4)),
+            pltpu.SemaphoreType.DMA((2, COMPS, 4)),
+            pltpu.SemaphoreType.DMA((2,)),
+            pltpu.SemaphoreType.DMA((2,)),
             pltpu.SemaphoreType.DMA((2, COMPS, 3)),
             pltpu.SemaphoreType.DMA((2, COMPS, 4)),
         ],

time: 80.4 us -> 77.6 us (0.965)
  the two profiles are of different devices: /device:TPU:11 before, /device:TPU:24 now
where the time goes in v3:
time: 77.6 us; the launch traced here: 77.5 us
  Pallas kernels  71.4 us (92%)
  local copies, waits for them, and re-layouts  5.4 us (7%)
    pallas_call x1, Pallas kernels, local(): pl.pallas_call(functools.partial(kernel, n_narrow, n_wide), out_shape=(pl...  71.4 us
    unnamed x2, local copies, waits for them, and re-layouts  5.4 us

profile of v3, /device:TPU:24, one launch (start us, length us, event | category | flops | bytes accessed | tf_op | source)
XLA Modules:
  0.0 77.5 jit_solution(3029111906508378750)
XLA Ops:
  0.6 71.4 %shard_map.50 = (f32[3,1024,128]{2,1,0:T(8,128)S(1)}, f32[3,7,8,32,512]{4,3,2,1,0:T(8,128)S(1)}) custom-call(f32[3,1024,1024]{2,1,0:T(8,128)} %bitcast.5, s32[7]{0:T(128)} %e_ref.1, bf16[3,2,512,256]{3,2,1,0:T(8,128)(2,1)} %constant.2.clone.w_ref), custom_call_target="tpu_custom_call" | custom-call | flops 10000000000 | bytes 26000000 | tf_op jit(solution)/shard_map/pallas_call | solution.py:603
  72.1 1.1 %copy.7 = f32[3,128,32,32]{1,3,2,0:T(8,128)} copy(f32[3,128,32,32]{1,3,2,0:T(8,128)S(1)} %bitcast.4) | data formatting | bytes 3145728
  73.2 4.3 %copy.8 = f32[3,7,8,32,512]{4,3,2,1,0:T(8,128)} copy(f32[3,7,8,32,512]{4,3,2,1,0:T(8,128)S(1)} %get-tuple-element.7) | data formatting | bytes 22020096

commit v4 on v3

--- a/solution.py
+++ b/solution.py
@@ -48,12 +48,72 @@
     return np.stack([head, rest], 1)
 
 
+def factor(e_ref, band):
+    shift = lax.shift_left(jnp.int32(1), 15 - e_ref[band - 1]).astype(F32)
+    ups = 2 - 2 * (band // 4) - 2 * ((band // 2) % 2)
+    return shift * (2.0**-15 * scaling**ups)
+
+
+def x_lift_quarter(cells, rims, e_ref, c, by, bz, put, low_put):
+    half = ROWS // 2
+    low_band, high_band = 2 * by + bz, 4 + 2 * by + bz
+    high_scale = factor(e_ref, high_band)
+    low_scale = factor(e_ref, low_band) if low_band else None
+
+    def body(at, carry):
+        k, t = at // 4, lax.rem(at, 4)
+        j = 4 * bz + k
+        row = pl.multiple_of(half * by + 8 * t, 8)
+
+        def plane(p):
+            return cells[j, pl.ds(pl.multiple_of(p * ROWS + row, 8), 8), :]
+
+        s = [plane(2 * i) for i in range(8)]
+        d = [plane(2 * i + 1) for i in range(8)]
+        pv = rims[0, c, 0, j, pl.ds(row, 8), :]
+        qv = rims[0, c, 1, j, pl.ds(row, 8), :]
+        sv = rims[1, c, 0, j, pl.ds(row, 8), :]
+        dv = rims[1, c, 1, j, pl.ds(row, 8), :]
+        s.append(sv)
+        d = [d[i] + pa * (s[i] + s[i + 1]) for i in range(8)]
+        dm = pv + pa * s[0]
+        sn = sv + ub * (d[7] + dv)
+        sm = qv + ub * dm
+        s = [s[i] + ub * ((d[i - 1] if i else dm) + d[i]) for i in range(8)]
+        dm = dm + pg * (sm + s[0])
+        s.append(sn)
+        d = [d[i] + pg * (s[i] + s[i + 1]) for i in range(8)]
+        s = [s[i] + ue * ((d[i - 1] if i else dm) + d[i]) for i in range(8)]
+        lanes = pl.ds(pl.multiple_of(128 * k, 128), 128)
+        rows = pl.ds(pl.multiple_of(8 * t, 8), 8)
+        for i in range(8):
+            v = d[i] * high_scale
+            put(high_band, i, rows, lanes, v - jnp.clip(v, -0.5, 0.5))
+            if low_band:
+                v = s[i] * low_scale
+                put(low_band, i, rows, lanes, v - jnp.clip(v, -0.5, 0.5))
+            else:
+                low_put(k, t, i, s[i] * (scaling * scaling))
+        return carry
+
+    lax.fori_loop(0, 16, body, 0)
+
+
+def turn_blocks(received, c, put):
+    def body(g, carry):
+        put(pl.ds(pl.multiple_of(128 * g, 128), 128), received[c, g].reshape((128, 128)).T)
+        return carry
+
+    lax.fori_loop(0, 8, body, 0)
+
+
 def kernel(
     n_narrow, n_wide,
-    x_ref, e_ref, w_ref, ap_ref, det_ref,
-    a_buf, b_buf, hl, wv, ys, yr, yz, xs, xr, ms, mr, lll, lsend, lmid, lrecv,
+    x_ref, e_ref, w_ref, ap_ref, det_ref, a_last, xr, lrecv,
+    a_first, a_second, b_buf, hl, wv, ys, yr, yz, xs, ms, mr, lll, lsend, lmid,
     load_sem, w_sem, y_send, y_recv, x_send, x_recv, m_send, m_recv, l_send, l_recv,
 ):
+    cells = (a_first, a_second, a_last)
     nar = lax.axis_index("narrow")
     wid = lax.axis_index("wide")
     up = lax.rem(nar + n_narrow - 1, n_narrow)
@@ -65,7 +125,7 @@
 
     def load(c, j):
         return pltpu.make_async_copy(
-            x_ref.at[c, :, pl.ds(128 * j, 128)], a_buf.at[c, j], load_sem.at[c, j]
+            x_ref.at[c, :, pl.ds(128 * j, 128)], cells[c].at[j], load_sem.at[c, j]
         )
 
     load_w = pltpu.make_async_copy(w_ref, wv, w_sem)
@@ -115,7 +175,7 @@
     def y_values(c):
         def body(j, carry):
             def row(r):
-                return a_buf[c, j, pl.ds(r, PLANES, stride=ROWS), :]
+                return cells[c][j, pl.ds(r, PLANES, stride=ROWS), :]
 
             r0, r1, r2 = row(0), row(1), row(2)
             e0, e1, e2, e3 = row(ROWS - 4), row(ROWS - 3), row(ROWS - 2), row(ROWS - 1)
@@ -171,7 +231,7 @@
             def put(j, value):
                 b_buf[c, j, pl.ds(base, TILE), :] = value
 
-            z_rows(TILE, lambda j: a_buf[c, j, pl.ds(base, TILE), :], put)
+            z_rows(TILE, lambda j: cells[c][j, pl.ds(base, TILE), :], put)
             return carry
 
         lax.fori_loop(0, count, body, 0)
@@ -207,8 +267,8 @@
     def y_plane(c, p, j):
         base = pl.multiple_of(p * ROWS, ROWS)
         s, d = y_rows(c, j, base, [yz[c, j, pl.ds(PLANES * kind + p, 1), :] for kind in range(4)])
-        a_buf[c, j, pl.ds(base, half), :] = s
-        a_buf[c, j, pl.ds(base + half, half), :] = d
+        cells[c][j, pl.ds(base, half), :] = s
+        cells[c][j, pl.ds(base + half, half), :] = d
 
     def y_rows(c, j, base, rim):
         s = b_buf[c, j, pl.ds(base, half, stride=2), :]
@@ -250,7 +310,7 @@
     def x_values(c):
         def body(j, carry):
             def plane(p):
-                return a_buf[c, j, p * ROWS : p * ROWS + ROWS, :]
+                return cells[c][j, p * ROWS : p * ROWS + ROWS, :]
 
             p0 = plane(0)
             xs[0, c, 0, j] = p0
@@ -266,7 +326,7 @@
         def body(j, carry):
 
             def plane(p):
-                return a_buf[c, j, p * ROWS : p * ROWS + ROWS, :]
+                return cells[c][j, p * ROWS : p * ROWS + ROWS, :]
 
             @pl.when(jnp.logical_not(has_left))
             def _():
@@ -378,53 +438,14 @@
         def _():
             side_lift(1)
 
-    def factor(band):
-        shift = lax.shift_left(jnp.int32(1), 15 - e_ref[band - 1]).astype(F32)
-        ups = 2 - 2 * (band // 4) - 2 * ((band // 2) % 2)
-        return shift * (2.0**-15 * scaling**ups)
-
     def x_lift(c, by, bz):
-        low_band, high_band = 2 * by + bz, 4 + 2 * by + bz
-        high_scale = factor(high_band)
-        low_scale = factor(low_band) if low_band else None
-
-        def body(at, carry):
-            k, t = at // 4, lax.rem(at, 4)
-            j = 4 * bz + k
-            row = pl.multiple_of(half * by + 8 * t, 8)
-
-            def plane(p):
-                return a_buf[c, j, pl.ds(pl.multiple_of(p * ROWS + row, 8), 8), :]
-
-            s = [plane(2 * i) for i in range(8)]
-            d = [plane(2 * i + 1) for i in range(8)]
-            pv = xr[0, c, 0, j, pl.ds(row, 8), :]
-            qv = xr[0, c, 1, j, pl.ds(row, 8), :]
-            sv = xr[1, c, 0, j, pl.ds(row, 8), :]
-            dv = xr[1, c, 1, j, pl.ds(row, 8), :]
-            s.append(sv)
-            d = [d[i] + pa * (s[i] + s[i + 1]) for i in range(8)]
-            dm = pv + pa * s[0]
-            sn = sv + ub * (d[7] + dv)
-            sm = qv + ub * dm
-            s = [s[i] + ub * ((d[i - 1] if i else dm) + d[i]) for i in range(8)]
-            dm = dm + pg * (sm + s[0])
-            s.append(sn)
-            d = [d[i] + pg * (s[i] + s[i + 1]) for i in range(8)]
-            s = [s[i] + ue * ((d[i - 1] if i else dm) + d[i]) for i in range(8)]
-            lanes = pl.ds(pl.multiple_of(128 * k, 128), 128)
-            rows = pl.ds(pl.multiple_of(8 * t, 8), 8)
-            for i in range(8):
-                v = d[i] * high_scale
-                det_ref[c, high_band - 1, i, rows, lanes] = v - jnp.clip(v, -0.5, 0.5)
-                if low_band:
-                    v = s[i] * low_scale
-                    det_ref[c, low_band - 1, i, rows, lanes] = v - jnp.clip(v, -0.5, 0.5)
-                else:
-                    lll[k, pl.ds(pl.multiple_of(half * i + 8 * t, 8), 8), :] = s[i] * (scaling * scaling)
-            return carry
-
-        lax.fori_loop(0, 16, body, 0)
+        def low_put(k, t, i, value):
+            lll[k, pl.ds(pl.multiple_of(half * i + 8 * t, 8), 8), :] = value
+
+        def put(band, i, rows, lanes, value):
+            det_ref[c, band - 1, i, rows, lanes] = value
+
+        x_lift_quarter(cells[c], xr, e_ref, c, by, bz, put, low_put)
 
     lane = lax.broadcasted_iota(jnp.int32, (8, 128), 1)
     low_half = lane < 64
@@ -490,16 +511,17 @@
             along(c, off, zpos).start()
         lrecv[c, :, :, zpos] = lmid[c, zpos]
 
-    def l_take(c):
+    def l_arrived(c):
         for off in (2, 1, 3):
             along(c, off, lax.rem(zpos + off, 4)).wait_recv()
 
-        def body(g, carry):
-            block = lrecv[c, g].reshape((128, 128))
-            ap_ref[c, pl.ds(pl.multiple_of(128 * g, 128), 128), :] = block.T
-            return carry
-
-        lax.fori_loop(0, 8, body, 0)
+    def l_take(c):
+        l_arrived(c)
+
+        def put(rows, value):
+            ap_ref[c, rows, :] = value
+
+        turn_blocks(lrecv, c, put)
 
     loaded(0)
     x_values(0)
@@ -562,9 +584,7 @@
     l_take(0)
     l_take(1)
     x_arrived(2, 2)
-    x_lift(2, 1, 0)
-    x_lift(2, 1, 1)
-    l_take(2)
+    l_arrived(2)
 
     for c in range(COMPS):
         @pl.when(has_up)
@@ -598,25 +618,71 @@
             along(c, off, zpos).wait_send()
 
 
+def finish(
+    e_ref, cells, rims, received, approx, details, approx_out, details_out,
+    last_details, last_approx, approx_sem, details_sem,
+):
+    c = COMPS - 1
+    bands = (2, 3, 6, 7)
+    early, late = [], {}
+    for comp in range(COMPS):
+        for band in range(1, 8):
+            mine = comp == c and band in bands
+            source = last_details.at[bands.index(band)] if mine else details.at[comp, band - 1]
+            copy = pltpu.make_async_copy(
+                source, details_out.at[comp, band - 1], details_sem.at[comp, band - 1]
+            )
+            if mine:
+                late[band] = copy
+            else:
+                early.append(copy)
+        copy = pltpu.make_async_copy(
+            last_approx if comp == c else approx.at[comp], approx_out.at[comp], approx_sem.at[comp]
+        )
+        if comp == c:
+            late[0] = copy
+        else:
+            early.append(copy)
+    for copy in early:
+        copy.start()
+
+    def put(band, i, rows, lanes, value):
+        last_details[bands.index(band), i, rows, lanes] = value
+
+    for bz in range(2):
+        x_lift_quarter(cells, rims, e_ref, c, 1, bz, put, None)
+        late[2 + bz].start()
+        late[6 + bz].start()
+
+    def put_block(rows, value):
+        last_approx[rows, :] = value
+
+    turn_blocks(received, c, put_block)
+    late[0].start()
+    for copy in early + list(late.values()):
+        copy.wait()
+
+
 def local(n_narrow, n_wide, velocity, exponents):
     cells = velocity.reshape((COMPS, PLANES * ROWS, DEPTH))
-    approx, details = pl.pallas_call(
+    approx, details, last, rims, received = pl.pallas_call(
         functools.partial(kernel, n_narrow, n_wide),
         out_shape=(
-            pltpu.VMEM((COMPS, 1024, 128), F32),
+            pltpu.VMEM((COMPS - 1, 1024, 128), F32),
             pltpu.VMEM((COMPS, 7, PLANES // 2, ROWS // 2, DEPTH // 2), F32),
+            pltpu.VMEM((CHUNKS, PLANES * ROWS, 128), F32),
+            pltpu.VMEM((2, COMPS, 2, CHUNKS, ROWS, 128), F32),
+            pltpu.VMEM((COMPS, 8, 4, 4, 8, 128), F32),
         ),
         in_specs=[
             pl.BlockSpec(memory_space=pl.ANY),
             pl.BlockSpec(memory_space=pltpu.SMEM),
             pl.BlockSpec(memory_space=pl.ANY),
         ],
-        out_specs=(
-            pl.BlockSpec(memory_space=pltpu.VMEM),
-            pl.BlockSpec(memory_space=pltpu.VMEM),
-        ),
+        out_specs=(pl.BlockSpec(memory_space=pltpu.VMEM),) * 5,
         scratch_shapes=[
-            pltpu.VMEM((COMPS, CHUNKS, PLANES * ROWS, 128), F32),
+            pltpu.VMEM((CHUNKS, PLANES * ROWS, 128), F32),
+            pltpu.VMEM((CHUNKS, PLANES * ROWS, 128), F32),
             pltpu.VMEM((COMPS, CHUNKS, PLANES * ROWS, 128), F32),
             pltpu.VMEM((2 * TILE + 32, DEPTH), BF16),
             pltpu.VMEM((3, 2, 512, 256), BF16),
@@ -624,13 +690,11 @@
             pltpu.VMEM((2, COMPS, CHUNKS, 2 * PLANES, 128), F32),
             pltpu.VMEM((COMPS, CHUNKS, 4 * PLANES, 128), F32),
             pltpu.VMEM((2, COMPS, 2, CHUNKS, ROWS, 128), F32),
-            pltpu.VMEM((2, COMPS, 2, CHUNKS, ROWS, 128), F32),
             pltpu.VMEM((2, CHUNKS, 8, 128), F32),
             pltpu.VMEM((2, CHUNKS, 8, 128), F32),
             pltpu.VMEM((4, 256, 128), F32),
             pltpu.VMEM((16, COMPS, 8, 8, 128), F32),
             pltpu.VMEM((COMPS, 4, 8, 4, 8, 128), F32),
-            pltpu.VMEM((COMPS, 8, 4, 4, 8, 128), F32),
             pltpu.SemaphoreType.DMA((COMPS, CHUNKS)),
             pltpu.SemaphoreType.DMA,
             pltpu.SemaphoreType.DMA((2, COMPS)),
@@ -643,12 +707,30 @@
             pltpu.SemaphoreType.DMA((2, COMPS, 4)),
         ],
         compiler_params=pltpu.CompilerParams(
-            collective_id=0, has_side_effects=True, vmem_limit_bytes=48 * 1024 * 1024
+            collective_id=0, has_side_effects=True, vmem_limit_bytes=38 * 1024 * 1024
         ),
         cost_estimate=pl.CostEstimate(
             flops=10_000_000_000, bytes_accessed=26_000_000, transcendentals=0
         ),
     )(cells, exponents, jnp.asarray(z_weights()))
+    approx, details = pl.pallas_call(
+        finish,
+        out_shape=(
+            jax.ShapeDtypeStruct((COMPS, 1024, 128), F32),
+            jax.ShapeDtypeStruct(details.shape, F32),
+        ),
+        in_specs=[pl.BlockSpec(memory_space=pltpu.SMEM)]
+        + [pl.BlockSpec(memory_space=pltpu.VMEM)] * 3
+        + [pl.BlockSpec(memory_space=pl.ANY)] * 2,
+        out_specs=(pl.BlockSpec(memory_space=pl.ANY),) * 2,
+        scratch_shapes=[
+            pltpu.VMEM((4, PLANES // 2, ROWS // 2, DEPTH // 2), F32),
+            pltpu.VMEM((1024, 128), F32),
+            pltpu.SemaphoreType.DMA((COMPS,)),
+            pltpu.SemaphoreType.DMA((COMPS, 7)),
+        ],
+        compiler_params=pltpu.CompilerParams(vmem_limit_bytes=4 * 1024 * 1024),
+    )(exponents, last, rims, received, approx, details)
     approx = approx.reshape((COMPS, ROWS // 2, 32, 128))
     return jnp.transpose(approx, (0, 3, 1, 2)), details
 

time: 77.6 us -> 75.4 us (0.972)
  local copies, waits for them, and re-layouts: 5.4 us -> 0.01 us
  Pallas kernels: 71.4 us -> 74.6 us
    unnamed x2, local copies, waits for them, and re-layouts: 5.4 us -> 0.01 us
    pallas_call x0 -> x1, Pallas kernels: none -> 5.29 us  [local(): pl.pallas_call(finish, out_shape=(jax.ShapeDtypeStruct((COMPS, 1024, 128)...]
    pallas_call x1, Pallas kernels: 71.4 us -> 69.3 us  [local(): pl.pallas_call(functools.partial(kernel, n_narrow, n_wide), out_shape=(pl...]
where the time goes in v4:
time: 75.4 us; the launch traced here: 75.3 us
  Pallas kernels  74.6 us (99%)
    pallas_call x1, Pallas kernels, local(): pl.pallas_call(functools.partial(kernel, n_narrow, n_wide), out_shape=(pl...  69.3 us
    pallas_call x1, Pallas kernels, local(): pl.pallas_call(finish, out_shape=(jax.ShapeDtypeStruct((COMPS, 1024, 128)...  5.29 us

profile of v4, /device:TPU:24, one launch (start us, length us, event | category | flops | bytes accessed | tf_op | source)
XLA Modules:
  0.0 75.3 jit_solution(6240390436751774189)
XLA Ops:
  0.6 0.0 copy-start
  0.6 69.3 %shard_map.50 = (f32[2,1024,128]{2,1,0:T(8,128)S(1)}, f32[3,7,8,32,512]{4,3,2,1,0:T(8,128)S(1)}, f32[8,1024,128]{2,1,0:T(8,128)S(1)}, f32[2,3,2,8,64,128]{5,4,3,2,1,0:T(8,128)S(1)}, f32[3,8,4,4,8,128]{5,4,3,2,1,0:T(8,128)S(1)}) custom-call(f32[3,1024,1024]{2,1,0:T(8,128)} %bitcast.4, s32[7]{0:T(128)} %e_ref.3, bf16[3,2,512,256]{3,2,1,0:T(8,128)(2,1)} %constant.2.clone.w_ref), custom_call_target="tpu_custom_call" | custom-call | flops 10000000000 | bytes 26000000 | tf_op jit(solution)/shard_map/pallas_call | solution.py:668
  70.0 0.0 copy-done
  70.0 5.3 %shard_map.51 = (f32[3,1024,128]{2,1,0:T(8,128)}, f32[3,7,8,32,512]{4,3,2,1,0:T(8,128)}) custom-call(s32[7]{0:T(128)S(1)} %copy-done, f32[8,1024,128]{2,1,0:T(8,128)S(1)} %get-tuple-element.9.cells, f32[2,3,2,8,64,128]{5,4,3,2,1,0:T(8,128)S(1)} %get-tuple-element.10.rims, f32[3,8,4,4,8,128]{5,4,3,2,1,0:T(8,128)S(1)} %get-tuple-element.11.received, ...), custom_call_target="tpu_custom_call" | custom-call | tf_op jit(solution)/shard_map/pallas_call | solution.py:716
Async XLA Ops:
  0.6 69.3 %copy-start = (s32[7]{0:T(128)S(1)}, s32[7]{0:T(128)}, u32[]{:S(2)}) copy-start(s32[7]{0:T(128)} %e_ref.3) | copy-start | bytes 88

commit v5 on v4

--- a/solution.py
+++ b/solution.py
@@ -111,7 +111,7 @@
     n_narrow, n_wide,
     x_ref, e_ref, w_ref, ap_ref, det_ref, a_last, xr, lrecv,
     a_first, a_second, b_buf, hl, wv, ys, yr, yz, xs, ms, mr, lll, lsend, lmid,
-    load_sem, w_sem, y_send, y_recv, x_send, x_recv, m_send, m_recv, l_send, l_recv,
+    load_sem, outer_sem, w_sem, y_send, y_recv, x_send, x_recv, m_send, m_recv, l_send, l_recv,
 ):
     cells = (a_first, a_second, a_last)
     nar = lax.axis_index("narrow")
@@ -128,20 +128,46 @@
             x_ref.at[c, :, pl.ds(128 * j, 128)], cells[c].at[j], load_sem.at[c, j]
         )
 
+    def load_outer(side, j):
+        rows = pl.ds(3 * TILE * side, TILE)
+        return pltpu.make_async_copy(
+            x_ref.at[0, rows, pl.ds(128 * j, 128)], cells[0].at[j, rows], outer_sem.at[side, j]
+        )
+
+    def load_inner(j):
+        rows = pl.ds(TILE, 2 * TILE)
+        return pltpu.make_async_copy(
+            x_ref.at[0, rows, pl.ds(128 * j, 128)], cells[0].at[j, rows], load_sem.at[0, j]
+        )
+
     load_w = pltpu.make_async_copy(w_ref, wv, w_sem)
     for j in range(CHUNKS):
-        load(0, j).start()
-    load_w.start()
+        load_outer(0, j).start()
+        load_outer(1, j).start()
+    for j in range(CHUNKS):
+        load_inner(j).start()
 
     barrier = pltpu.get_barrier_semaphore()
 
     def greet(off, carry):
-        pl.semaphore_signal(
-            barrier, inc=1, device_id={"wide": lax.rem(wid + off, n_wide)}, device_id_type=MESH
-        )
+        for peer in (
+            4 * lax.rem(wid // 4 + off, 4) + lax.rem(wid, 4),
+            4 * (wid // 4) + lax.rem(wid + off, 4),
+        ):
+            pl.semaphore_signal(barrier, inc=1, device_id={"wide": peer}, device_id_type=MESH)
         return carry
 
-    lax.fori_loop(1, n_wide, greet, 0)
+    lax.fori_loop(1, 4, greet, 0)
+    turn_left = jnp.logical_and(lax.rem(wid, 4) == 0, has_left)
+    turn_right = jnp.logical_and(lax.rem(wid, 4) == 3, has_right)
+
+    @pl.when(turn_left)
+    def _():
+        pl.semaphore_signal(barrier, inc=1, device_id={"wide": left}, device_id_type=MESH)
+
+    @pl.when(turn_right)
+    def _():
+        pl.semaphore_signal(barrier, inc=1, device_id={"wide": right}, device_id_type=MESH)
 
     @pl.when(has_up)
     def _():
@@ -152,7 +178,12 @@
         pl.semaphore_signal(barrier, inc=1, device_id={"narrow": down}, device_id_type=MESH)
 
     pl.semaphore_wait(
-        barrier, n_wide - 1 + has_up.astype(jnp.int32) + has_down.astype(jnp.int32)
+        barrier,
+        6
+        + turn_left.astype(jnp.int32)
+        + turn_right.astype(jnp.int32)
+        + has_up.astype(jnp.int32)
+        + has_down.astype(jnp.int32),
     )
 
     def y_copy(side, c):
@@ -167,7 +198,7 @@
 
     def loaded(c):
         for j in range(CHUNKS):
-            load(c, j).wait()
+            (load(c, j) if c else load_inner(j)).wait()
         if c + 1 < COMPS:
             for j in range(CHUNKS):
                 load(c + 1, j).start()
@@ -523,9 +554,13 @@
 
         turn_blocks(lrecv, c, put)
 
-    loaded(0)
+    for j in range(CHUNKS):
+        load_outer(0, j).wait()
+        load_outer(1, j).wait()
     x_values(0)
     x_start(0, 3)
+    loaded(0)
+    load_w.start()
     loaded(1)
     y_values(1)
     y_values(0)
@@ -696,6 +731,7 @@
             pltpu.VMEM((16, COMPS, 8, 8, 128), F32),
             pltpu.VMEM((COMPS, 4, 8, 4, 8, 128), F32),
             pltpu.SemaphoreType.DMA((COMPS, CHUNKS)),
+            pltpu.SemaphoreType.DMA((2, CHUNKS)),
             pltpu.SemaphoreType.DMA,
             pltpu.SemaphoreType.DMA((2, COMPS)),
             pltpu.SemaphoreType.DMA((2, COMPS)),

time: 75.4 us -> 74.5 us (0.988)
  Pallas kernels: 74.6 us -> 73.2 us
    pallas_call x1, Pallas kernels: 69.3 us -> 68 us  [local(): pl.pallas_call(functools.partial(kernel, n_narrow, n_wide), out_shape=(pl...]
where the time goes in v5:
time: 74.5 us; the launch traced here: 73.9 us
  Pallas kernels  73.2 us (98%)
    pallas_call x1, Pallas kernels, local(): pl.pallas_call(functools.partial(kernel, n_narrow, n_wide), out_shape=(pl...  68 us
    pallas_call x1, Pallas kernels, local(): pl.pallas_call(finish, out_shape=(jax.ShapeDtypeStruct((COMPS, 1024, 128)...  5.29 us

profile of v5, /device:TPU:24, one launch (start us, length us, event | category | flops | bytes accessed | tf_op | source)
XLA Modules:
  0.0 73.9 jit_solution(16241439661072834968)
XLA Ops:
  0.6 0.0 copy-start
  0.6 68.0 %shard_map.50 = (f32[2,1024,128]{2,1,0:T(8,128)S(1)}, f32[3,7,8,32,512]{4,3,2,1,0:T(8,128)S(1)}, f32[8,1024,128]{2,1,0:T(8,128)S(1)}, f32[2,3,2,8,64,128]{5,4,3,2,1,0:T(8,128)S(1)}, f32[3,8,4,4,8,128]{5,4,3,2,1,0:T(8,128)S(1)}) custom-call(f32[3,1024,1024]{2,1,0:T(8,128)} %bitcast.4, s32[7]{0:T(128)} %e_ref.3, bf16[3,2,512,256]{3,2,1,0:T(8,128)(2,1)} %constant.2.clone.w_ref), custom_call_target="tpu_custom_call" | custom-call | flops 10000000000 | bytes 26000000 | tf_op jit(solution)/shard_map/pallas_call | solution.py:703
  68.6 0.0 copy-done
  68.6 5.3 %shard_map.51 = (f32[3,1024,128]{2,1,0:T(8,128)}, f32[3,7,8,32,512]{4,3,2,1,0:T(8,128)}) custom-call(s32[7]{0:T(128)S(1)} %copy-done, f32[8,1024,128]{2,1,0:T(8,128)S(1)} %get-tuple-element.9.cells, f32[2,3,2,8,64,128]{5,4,3,2,1,0:T(8,128)S(1)} %get-tuple-element.10.rims, f32[3,8,4,4,8,128]{5,4,3,2,1,0:T(8,128)S(1)} %get-tuple-element.11.received, ...), custom_call_target="tpu_custom_call" | custom-call | tf_op jit(solution)/shard_map/pallas_call | solution.py:752
Async XLA Ops:
  0.6 68.0 %copy-start = (s32[7]{0:T(128)S(1)}, s32[7]{0:T(128)}, u32[]{:S(2)}) copy-start(s32[7]{0:T(128)} %e_ref.3) | copy-start | bytes 88

commit v6 on v5

--- a/solution.py
+++ b/solution.py
@@ -144,8 +144,6 @@
     for j in range(CHUNKS):
         load_outer(0, j).start()
         load_outer(1, j).start()
-    for j in range(CHUNKS):
-        load_inner(j).start()
 
     barrier = pltpu.get_barrier_semaphore()
 
@@ -177,14 +175,8 @@
     def _():
         pl.semaphore_signal(barrier, inc=1, device_id={"narrow": down}, device_id_type=MESH)
 
-    pl.semaphore_wait(
-        barrier,
-        6
-        + turn_left.astype(jnp.int32)
-        + turn_right.astype(jnp.int32)
-        + has_up.astype(jnp.int32)
-        + has_down.astype(jnp.int32),
-    )
+    for j in range(CHUNKS):
+        load_inner(j).start()
 
     def y_copy(side, c):
         return pltpu.make_async_remote_copy(
@@ -558,6 +550,14 @@
         load_outer(0, j).wait()
         load_outer(1, j).wait()
     x_values(0)
+    pl.semaphore_wait(
+        barrier,
+        6
+        + turn_left.astype(jnp.int32)
+        + turn_right.astype(jnp.int32)
+        + has_up.astype(jnp.int32)
+        + has_down.astype(jnp.int32),
+    )
     x_start(0, 3)
     loaded(0)
     load_w.start()

time: 74.5 us -> 73.8 us (level)
  no operation moved by 1% of the time
where the time goes in v6:
time: 73.8 us; the launch traced here: 73.5 us
  Pallas kernels  72.9 us (99%)
    pallas_call x1, Pallas kernels, local(): pl.pallas_call(functools.partial(kernel, n_narrow, n_wide), out_shape=(pl...  67.6 us
    pallas_call x1, Pallas kernels, local(): pl.pallas_call(finish, out_shape=(jax.ShapeDtypeStruct((COMPS, 1024, 128)...  5.29 us

profile of v6, /device:TPU:24, one launch (start us, length us, event | category | flops | bytes accessed | tf_op | source)
XLA Modules:
  0.0 73.5 jit_solution(149211855253428241)
XLA Ops:
  0.6 0.0 copy-start
  0.6 67.6 %shard_map.50 = (f32[2,1024,128]{2,1,0:T(8,128)S(1)}, f32[3,7,8,32,512]{4,3,2,1,0:T(8,128)S(1)}, f32[8,1024,128]{2,1,0:T(8,128)S(1)}, f32[2,3,2,8,64,128]{5,4,3,2,1,0:T(8,128)S(1)}, f32[3,8,4,4,8,128]{5,4,3,2,1,0:T(8,128)S(1)}) custom-call(f32[3,1024,1024]{2,1,0:T(8,128)} %bitcast.4, s32[7]{0:T(128)} %e_ref.3, bf16[3,2,512,256]{3,2,1,0:T(8,128)(2,1)} %constant.2.clone.w_ref), custom_call_target="tpu_custom_call" | custom-call | flops 10000000000 | bytes 26000000 | tf_op jit(solution)/shard_map/pallas_call | solution.py:703
  68.2 0.0 copy-done
  68.2 5.3 %shard_map.51 = (f32[3,1024,128]{2,1,0:T(8,128)}, f32[3,7,8,32,512]{4,3,2,1,0:T(8,128)}) custom-call(s32[7]{0:T(128)S(1)} %copy-done, f32[8,1024,128]{2,1,0:T(8,128)S(1)} %get-tuple-element.9.cells, f32[2,3,2,8,64,128]{5,4,3,2,1,0:T(8,128)S(1)} %get-tuple-element.10.rims, f32[3,8,4,4,8,128]{5,4,3,2,1,0:T(8,128)S(1)} %get-tuple-element.11.received, ...), custom_call_target="tpu_custom_call" | custom-call | tf_op jit(solution)/shard_map/pallas_call | solution.py:752
Async XLA Ops:
  0.6 67.6 %copy-start = (s32[7]{0:T(128)S(1)}, s32[7]{0:T(128)}, u32[]{:S(2)}) copy-start(s32[7]{0:T(128)} %e_ref.3) | copy-start | bytes 88
